TPU v7x, 768 devices: a whole 4x8x12 slice. The times are simulated.
768 devices in a mesh: lon: 16 (over x, y_lo), lat: 48 (over z, y_hi, core).
Axes of the slice: x: 4, y: 8 (y_hi: 2, y_lo: 4; y = y_hi * 4 + y_lo), z: 12, core: 2. Of those that a mesh axis runs over, the one named last changes fastest.
Arguments:
- cotangent: float32 [2, 16, 1536, 4096], P(None, None, 'lat', 'lon'), may hold values from -6 to 6
- east_velocity: float32 [16, 1536, 4096], P(None, 'lat', 'lon'), may hold values from -1.8 to 1.8
- north_velocity: float32 [16, 1536, 4096], P(None, 'lat', 'lon'), may hold values from -1.8 to 1.8
- diffusivity: float32 [16, 1536, 4096], P(None, 'lat', 'lon'), may hold values from 0.02 to 0.12
- vertical_diffusivity: float32 [16, 1536, 4096], P(None, 'lat', 'lon'), may hold values from 0.02 to 0.2
- cell_mask: int32 [1536, 4096], P('lat', 'lon'), may hold values from 0 to 65535, as said below
- east_mask: int32 [1536, 4096], P('lat', 'lon'), may hold values from 0 to 65535, as said below
- north_mask: int32 [1536, 4096], P('lat', 'lon'), may hold values from 0 to 65535, as said below
- fold_partner: int32 [4096], P('lon'), may hold values from 0 to 4095, as said below
Outputs:
- initial_adjoint: float32 [2, 16, 1536, 4096], P(None, None, 'lat', 'lon')
Inputs may be any that keep to these rules, and one draw needn't show every extreme that they name: `cell_mask`: bit k is set for the sea levels of a column, which run from level 0 down to a bottom level; land columns are 0. `east_mask`: equals cell_mask of the cell AND cell_mask of the next column, periodic in longitude. `north_mask`: equals cell_mask of the cell AND cell_mask of the next row; on the last row AND cell_mask of the last row at column fold_partner[i]. fold_partner[i] = (c - i) mod 4096 for one whole number c, so fold_partner[fold_partner[i]] = i.
All inputs are finite; a program needn't handle non-finite values.
Results may differ from a plain program's by a relative error of at most 0.0003.
Values sent between devices are 32-bit elements; how exact they have to be, the bound alone decides.
A program may use at most 64 MiB of HBM per device.

v0:
```python
import jax
import jax.numpy as jnp
from jax import lax
from jax.sharding import PartitionSpec as P

STEPS = 2


def shifted(value, axis, steps):
    count = lax.axis_size(axis)
    pairs = [(source, (source + steps) % count) for source in range(count)]
    return lax.ppermute(value, axis, pairs)


def passed_along(array, axis, by):
    length = lax.axis_size(axis)
    pairs = [(i, i + by) for i in range(length) if 0 <= i + by < length]
    return lax.ppermute(array, axis, pairs)


def unpack_levels(packed_words, levels):
    level_bits = jnp.arange(levels, dtype=jnp.int32)[:, None, None]
    return jnp.bitwise_and(jnp.right_shift(packed_words[None], level_bits), 1).astype(jnp.float32)


def select_partner(partner_cols, piece_rows):
    width = piece_rows.shape[1]
    inside = jnp.logical_and(partner_cols >= 0, partner_cols < width)
    picked = jnp.take(piece_rows, jnp.clip(partner_cols, 0, width - 1), axis=1)
    return jnp.where(inside[None, :], picked, 0.0)


def per_device(
    cotangent,
    east_velocity,
    north_velocity,
    diffusivity,
    vertical_diffusivity,
    cell_mask,
    east_mask,
    north_mask,
    fold_partner,
):
    levels = cotangent.shape[1]
    lat_rows = cotangent.shape[2]
    lon_cols = cotangent.shape[3]
    cell_open = unpack_levels(cell_mask, levels)
    east_open = unpack_levels(east_mask, levels)
    north_open = unpack_levels(north_mask, levels)
    east_plus = east_open * (0.5 * east_velocity + diffusivity)
    east_minus = east_open * (0.5 * east_velocity - diffusivity)
    north_plus = north_open * (0.5 * north_velocity + diffusivity)
    north_minus = north_open * (0.5 * north_velocity - diffusivity)
    vertical = vertical_diffusivity[:-1] * cell_open[:-1] * cell_open[1:]
    lat_last = lax.axis_index("lat") == lax.axis_size("lat") - 1
    row_iota = lax.broadcasted_iota(jnp.int32, (lat_rows, 1), 0)
    top_row = jnp.logical_and(row_iota == lat_rows - 1, lat_last)
    tracer = cotangent
    for repeat in range(STEPS):
        masked = cell_open * tracer
        level_flux = vertical * (masked[:, 1:] - masked[:, :-1])
        zero_level = jnp.zeros_like(masked[:, :1])
        result = (
            masked
            + jnp.concatenate([level_flux, zero_level], axis=1)
            - jnp.concatenate([zero_level, level_flux], axis=1)
        )
        east_next = shifted(masked[:, :, :, :1], "lon", -1)
        east_diff = jnp.concatenate([masked[:, :, :, 1:], east_next], axis=3) - masked
        east_push = east_minus * east_diff
        from_west = shifted(east_push[:, :, :, -1:], "lon", 1)
        result = (
            result
            + east_plus * east_diff
            + jnp.concatenate([from_west, east_push[:, :, :, :-1]], axis=3)
        )
        north_next = passed_along(masked[:, :, :1, :], "lat", -1)
        north_diff = jnp.concatenate([masked[:, :, 1:, :], north_next], axis=2) - masked
        north_push = north_minus * north_diff
        from_south = passed_along(north_push[:, :, -1:, :], "lat", 1)
        result = (
            result
            + north_plus * north_diff
            + jnp.concatenate([from_south, north_push[:, :, :-1, :]], axis=2)
        )
        fold_terms = north_push[:, :, -1, :]
        top_terms = fold_terms.reshape(2 * levels, lon_cols)
        returned = select_partner(
            fold_partner, lax.all_gather(top_terms, "lon", axis=1, tiled=True)
        )
        returned = returned.reshape(2, levels, 1, lon_cols)
        tracer = result + jnp.where(top_row, returned, 0.0)
    return tracer


def solution(mesh):
    placed = (
        P(None, None, "lat", "lon"),
        P(None, "lat", "lon"),
        P(None, "lat", "lon"),
        P(None, "lat", "lon"),
        P(None, "lat", "lon"),
        P("lat", "lon"),
        P("lat", "lon"),
        P("lat", "lon"),
        P("lon"),
    )
    return jax.shard_map(
        per_device,
        mesh=mesh,
        in_specs=placed,
        out_specs=P(None, None, "lat", "lon"),
        check_vma=False,
    )
```

profile of v0, /device:TPU:1, one launch (start us, length us, event | category | flops | bytes accessed | tf_op | source)
XLA Modules:
  0.0 234.2 jit_solution(3108164652076602614)
XLA Ops:
  0.0 0.9 and_convert_fusion
  0.9 0.3 copy.14
  1.2 0.0 copy-done
  1.2 0.0 copy-start.18
  1.3 0.0 copy-start.15
  1.3 0.7 copy_multiply_fusion
  1.9 0.8 slice.103
  2.8 8.2 %collective-permute-start = (f32[2,16,32,1]{3,1,0,2:T(8,128)}, f32[2,16,32,1]{3,1,0,2:T(8,128)}, u32[]{:S(2)}, u32[]{:S(2)}) collective-permute-start(f32[2,16,32,1]{3,1,0,2:T(8,128)} %slice.103), channel_id=1, source_target_pairs={{0,720},{48,0},{96,48},{144,96},{192,144},{240,192},{288,240},{336... | collective-permute-start | bytes 12296 | tf_op jit(solution)/shard_map/ppermute | solution.py:12
  11.0 6.1 %collective-permute-start.2 = (f32[2,16,1,256]{3,1,0,2:T(8,128)S(1)}, f32[2,16,1,256]{3,1,0,2:T(8,128)S(1)}, u32[]{:S(2)}, u32[]{:S(2)}) collective-permute-start(f32[2,16,1,256]{3,1,0,2:T(8,128)S(1)} %slice.107), channel_id=1, source_target_pairs={{1,0},{2,1},{3,2},{4,3},{5,4},{6,5},{7,6},{8,7},{9,8},{10,9},{11,1... | collective-permute-start | bytes 98312 | tf_op jit(solution)/shard_map/ppermute | solution.py:18
  17.2 0.0 copy-done.15
  17.2 0.1 slice_multiply_fusion
  17.3 0.0 copy-start.16
  17.3 0.0 copy-start.17
  17.3 0.3 copy.16
  17.6 0.0 copy-start.14
  17.6 1.2 fusion.1
  18.8 0.0 copy-done.16
  18.8 0.2 copy-done.14
  19.1 1.5 add_multiply_fusion.1
  20.6 0.3 slice.102
  20.9 0.1 slice.106
  21.0 0.3 copy.18
  21.4 0.3 copy.20
  21.7 1.1 copy.17
  22.8 1.1 copy.19
  23.9 0.0 collective-permute-done
  24.0 3.0 %collective-permute-done.2 = f32[2,16,1,256]{3,1,0,2:T(8,128)S(1)} collective-permute-done((f32[2,16,1,256]{3,1,0,2:T(8,128)S(1)}, f32[2,16,1,256]{3,1,0,2:T(8,128)S(1)}, u32[]{:S(2)}, u32[]{:S(2)}) %collective-permute-start.2) | collective-permute-done | bytes 32800 | tf_op jit(solution)/shard_map/ppermute | solution.py:18
  27.0 2.1 broadcast_multiply_fusion.1
  29.1 0.0 copy-start.4
  29.1 0.9 copy-done.11
  30.0 1.9 collective-permute-start.3
  32.0 0.1 copy.21
  32.1 64.7 %all_gather.6 = f32[32,4096]{0,1:T(8,128)} all-gather(f32[32,256]{0,1:T(8,128)S(1)} %copy.21), channel_id=1, replica_groups=mesh['lon'=16,'lat'=48] {'lon'}, dimensions={1}, use_global_device_ids=true | all-gather | bytes 557056 | tf_op jit(solution)/shard_map/all_gather | solution.py:89
  96.8 1.0 slice.104
  97.8 1.9 collective-permute-start.1
  99.7 2.3 gather_fusion
  102.0 0.1 bitcast_select_fusion.1
  102.2 2.3 slice.109
  104.5 0.1 copy.22
  104.5 12.5 %collective-permute-done.1 = f32[2,16,32,1]{3,1,0,2:T(8,128)} collective-permute-done((f32[2,16,32,1]{3,1,0,2:T(8,128)}, f32[2,16,32,1]{3,1,0,2:T(8,128)}, u32[]{:S(2)}, u32[]{:S(2)}) %collective-permute-start.1) | collective-permute-done | bytes 4128 | tf_op jit(solution)/shard_map/ppermute | solution.py:12
  117.0 0.0 collective-permute-done.3
  117.0 4.9 %fusion.5 = f32[2,16,32,256]{3,1,0,2:T(8,128)S(1)} fusion(f32[2,16,32,255]{3,1,0,2:T(8,128)} %bitcast.10, f32[2,16,32,1]{3,1,0,2:T(8,128)} %collective-permute-done.1, f32[2,16,31,256]{3,1,0,2:T(8,128)} %slice.109, f32[2,16,1,256]{3,1,0,2:T(8,128)S(1)} %collective-permute-done.3, f32[2,15,32,256]{3,1,0,2:T(8,128)} %fusion.1, f32[2,16,256]{2,1,0:T(8,128)S(1)} %bitcast.13, ...), kind=kLoop, calls=%fused_computation.11 | loop fusion | flops 4718592 | bytes 8880160 | tf_op jit(solution)/shard_map/mul | solution.py:60
  121.9 1.9 collective-permute-start.4
  123.9 3.2 %collective-permute-start.6 = (f32[2,16,1,256]{3,1,0,2:T(8,128)S(1)}, f32[2,16,1,256]{3,1,0,2:T(8,128)S(1)}, u32[]{:S(2)}, u32[]{:S(2)}) collective-permute-start(f32[2,16,1,256]{3,1,0,2:T(8,128)S(1)} %slice.117), channel_id=1, source_target_pairs={{1,0},{2,1},{3,2},{4,3},{5,4},{6,5},{7,6},{8,7},{9,8},{10,9},{11,1... | collective-permute-start | bytes 98312 | tf_op jit(solution)/shard_map/ppermute | solution.py:18
  127.1 1.2 fusion
  128.3 0.3 slice.112
  128.7 0.1 slice.116
  128.8 7.9 %collective-permute-done.4 = f32[2,16,32,1]{3,1,0,2:T(8,128)S(1)} collective-permute-done((f32[2,16,32,1]{3,1,0,2:T(8,128)S(1)}, f32[2,16,32,1]{3,1,0,2:T(8,128)S(1)}, u32[]{:S(2)}, u32[]{:S(2)}) %collective-permute-start.4) | collective-permute-done | bytes 4128 | tf_op jit(solution)/shard_map/ppermute | solution.py:12
  136.6 3.3 %collective-permute-done.6 = f32[2,16,1,256]{3,1,0,2:T(8,128)S(1)} collective-permute-done((f32[2,16,1,256]{3,1,0,2:T(8,128)S(1)}, f32[2,16,1,256]{3,1,0,2:T(8,128)S(1)}, u32[]{:S(2)}, u32[]{:S(2)}) %collective-permute-start.6) | collective-permute-done | bytes 32800 | tf_op jit(solution)/shard_map/ppermute | solution.py:18
  139.9 1.6 broadcast_multiply_fusion
  141.5 1.0 copy-done.12
  142.4 3.5 %collective-permute-start.7 = (f32[2,16,1,256]{3,1,0,2:T(8,128)S(1)}, f32[2,16,1,256]{3,1,0,2:T(8,128)S(1)}, u32[]{:S(2)}, u32[]{:S(2)}) collective-permute-start(f32[2,16,1,256]{3,1,0,2:T(8,128)S(1)} %slice.118), channel_id=1, source_target_pairs={{0,1},{1,2},{2,3},{3,4},{4,5},{5,6},{6,7},{7,8},{8,9},{9,10},{10,1... | collective-permute-start | bytes 98312 | tf_op jit(solution)/shard_map/ppermute | solution.py:18
  146.0 0.1 copy.23
  146.1 62.5 %all_gather.7 = f32[32,4096]{0,1:T(8,128)} all-gather(f32[32,256]{0,1:T(8,128)S(1)} %copy.23), channel_id=1, replica_groups=mesh['lon'=16,'lat'=48] {'lon'}, dimensions={1}, use_global_device_ids=true | all-gather | bytes 557056 | tf_op jit(solution)/shard_map/all_gather | solution.py:89
  208.6 2.3 gather_fusion.1
  210.9 2.0 slice.114
  212.9 1.9 collective-permute-start.5
  214.8 0.1 bitcast_select_fusion
  215.0 2.3 slice.119
  217.3 0.1 copy.24
  217.3 11.2 %collective-permute-done.5 = f32[2,16,32,1]{3,1,0,2:T(8,128)} collective-permute-done((f32[2,16,32,1]{3,1,0,2:T(8,128)}, f32[2,16,32,1]{3,1,0,2:T(8,128)}, u32[]{:S(2)}, u32[]{:S(2)}) %collective-permute-start.5) | collective-permute-done | bytes 4128 | tf_op jit(solution)/shard_map/ppermute | solution.py:12
  228.6 0.0 collective-permute-done.7
  228.6 4.0 %fusion.8 = f32[2,16,32,256]{3,1,0,2:T(8,128)S(1)} fusion(f32[2,16,32,255]{3,1,0,2:T(8,128)} %bitcast.11, f32[2,16,32,1]{3,1,0,2:T(8,128)} %collective-permute-done.5, f32[2,16,31,256]{3,1,0,2:T(8,128)} %slice.119, f32[2,16,1,256]{3,1,0,2:T(8,128)S(1)} %collective-permute-done.7, f32[2,15,32,256]{3,1,0,2:T(8,128)} %fusion, f32[2,16,32,256]{3,1,0,2:T(8,128)S(1)} %fusion.5, ...), kind=kLoop, calls=%fused_computation.17 | loop fusion | flops 4194304 | bytes 8355872 | tf_op jit(solution)/shard_map/add | solution.py:92
  232.6 1.6 copy.25
  (35 shorter events, 0.1 us)
Async XLA Ops:
  0.0 1.2 copy-start
  1.2 16.0 %copy-start.2 = (f32[16,32,256]{2,0,1:T(8,128)}, f32[16,32,256]{2,0,1:T(8,128)S(1)}, u32[]{:S(2)}) copy-start(f32[16,32,256]{2,0,1:T(8,128)S(1)} %copy.14) | copy-start | bytes 1572868
  1.2 15.9 %copy-start.18 = (s32[256]{0:T(256)S(1)}, s32[256]{0:T(256)}, u32[]{:S(2)}) copy-start(s32[256]{0:T(256)} %param.19) | copy-start | bytes 3076
  1.3 15.9 %copy-start.15 = (f32[16,32,256]{2,1,0:T(8,128)S(1)}, f32[16,32,256]{2,1,0:T(8,128)}, u32[]{:S(2)}) copy-start(f32[16,32,256]{2,1,0:T(8,128)} %param.15) | copy-start | bytes 1572868
  2.8 21.2 %collective-permute-start = (f32[2,16,32,1]{3,1,0,2:T(8,128)}, f32[2,16,32,1]{3,1,0,2:T(8,128)}, u32[]{:S(2)}, u32[]{:S(2)}) collective-permute-start(f32[2,16,32,1]{3,1,0,2:T(8,128)} %slice.103), channel_id=1, source_target_pairs={{0,720},{48,0},{96,48},{144,96},{192,144},{240,192},{288,240},{336... | collective-permute-start | bytes 12296 | tf_op jit(solution)/shard_map/ppermute | solution.py:12
  11.0 15.9 %collective-permute-start.2 = (f32[2,16,1,256]{3,1,0,2:T(8,128)S(1)}, f32[2,16,1,256]{3,1,0,2:T(8,128)S(1)}, u32[]{:S(2)}, u32[]{:S(2)}) collective-permute-start(f32[2,16,1,256]{3,1,0,2:T(8,128)S(1)} %slice.107), channel_id=1, source_target_pairs={{1,0},{2,1},{3,2},{4,3},{5,4},{6,5},{7,6},{8,7},{9,8},{10,9},{11,1... | collective-permute-start | bytes 98312 | tf_op jit(solution)/shard_map/ppermute | solution.py:18
  17.3 1.5 copy-start.16
  17.3 1.5 copy-start.17
  17.6 3.0 %copy-start.5 = (f32[15,32,256]{2,0,1:T(8,128)}, f32[15,32,256]{2,0,1:T(8,128)S(1)}, u32[]{:S(2)}) copy-start(f32[15,32,256]{2,0,1:T(8,128)S(1)} %copy.16) | copy-start | bytes 1474564
  17.6 1.4 copy-start.14
  21.0 5.9 %copy-start.1 = (f32[2,16,31,256]{3,1,0,2:T(8,128)}, f32[2,16,31,256]{3,1,0,2:T(8,128)S(1)}, u32[]{:S(2)}) copy-start(f32[2,16,31,256]{3,1,0,2:T(8,128)S(1)} %slice.106) | copy-start | bytes 3047428
  21.0 5.9 %copy-start.3 = (f32[16,32,256]{2,0,1:T(8,128)S(1)}, f32[16,32,256]{2,0,1:T(8,128)}, u32[]{:S(2)}) copy-start(f32[16,32,256]{2,0,1:T(8,128)} %copy-done.2) | copy-start | bytes 1572868
  21.4 7.7 %copy-start.7 = (f32[16,32,256]{2,0,1:T(8,128)}, f32[16,32,256]{2,0,1:T(8,128)S(1)}, u32[]{:S(2)}) copy-start(f32[16,32,256]{2,0,1:T(8,128)S(1)} %copy.18) | copy-start | bytes 1572868
  21.7 7.4 %copy-start.9 = (f32[16,32,256]{2,0,1:T(8,128)}, f32[16,32,256]{2,0,1:T(8,128)S(1)}, u32[]{:S(2)}) copy-start(f32[16,32,256]{2,0,1:T(8,128)S(1)} %copy.20) | copy-start | bytes 1572868
  29.1 1.0 copy-start.11
  29.1 75.4 %copy-start.4 = (f32[2,16,32,256]{3,1,0,2:T(8,128)}, f32[2,16,32,256]{3,1,0,2:T(8,128)S(1)}, u32[]{:S(2)}) copy-start(f32[2,16,32,256]{3,1,0,2:T(8,128)S(1)} %get-tuple-element.13) | copy-start | bytes 3145732
  30.0 87.0 %collective-permute-start.3 = (f32[2,16,1,256]{3,1,0,2:T(8,128)S(1)}, f32[2,16,1,256]{3,1,0,2:T(8,128)S(1)}, u32[]{:S(2)}, u32[]{:S(2)}) collective-permute-start(f32[2,16,1,256]{3,1,0,2:T(8,128)S(1)} %slice.108), channel_id=1, source_target_pairs={{0,1},{1,2},{2,3},{3,4},{4,5},{5,6},{6,7},{7,8},{8,9},{9,10},{10,1... | collective-permute-start | bytes 98312 | tf_op jit(solution)/shard_map/ppermute | solution.py:18
  97.8 19.2 %collective-permute-start.1 = (f32[2,16,32,1]{3,1,0,2:T(8,128)}, f32[2,16,32,1]{3,1,0,2:T(8,128)}, u32[]{:S(2)}, u32[]{:S(2)}) collective-permute-start(f32[2,16,32,1]{3,1,0,2:T(8,128)} %slice.104), channel_id=1, source_target_pairs={{0,48},{48,96},{96,144},{144,192},{192,240},{240,288},{288,336},{3... | collective-permute-start | bytes 12296 | tf_op jit(solution)/shard_map/ppermute | solution.py:12
  117.0 10.1 %copy-start.6 = (f32[15,32,256]{2,0,1:T(8,128)S(1)}, f32[15,32,256]{2,0,1:T(8,128)}, u32[]{:S(2)}) copy-start(f32[15,32,256]{2,0,1:T(8,128)} %copy-done.5) | copy-start | bytes 1474564
  121.9 14.7 %collective-permute-start.4 = (f32[2,16,32,1]{3,1,0,2:T(8,128)S(1)}, f32[2,16,32,1]{3,1,0,2:T(8,128)S(1)}, u32[]{:S(2)}, u32[]{:S(2)}) collective-permute-start(f32[2,16,32,1]{3,1,0,2:T(8,128)S(1)} %slice.113), channel_id=1, source_target_pairs={{0,720},{48,0},{96,48},{144,96},{192,144},{240,192},{288,240},{336... | collective-permute-start | bytes 12296 | tf_op jit(solution)/shard_map/ppermute | solution.py:12
  123.9 16.0 %collective-permute-start.6 = (f32[2,16,1,256]{3,1,0,2:T(8,128)S(1)}, f32[2,16,1,256]{3,1,0,2:T(8,128)S(1)}, u32[]{:S(2)}, u32[]{:S(2)}) collective-permute-start(f32[2,16,1,256]{3,1,0,2:T(8,128)S(1)} %slice.117), channel_id=1, source_target_pairs={{1,0},{2,1},{3,2},{4,3},{5,4},{6,5},{7,6},{8,7},{9,8},{10,9},{11,1... | collective-permute-start | bytes 98312 | tf_op jit(solution)/shard_map/ppermute | solution.py:18
  128.3 11.6 %copy-start.8 = (f32[16,32,256]{2,0,1:T(8,128)S(1)}, f32[16,32,256]{2,0,1:T(8,128)}, u32[]{:S(2)}) copy-start(f32[16,32,256]{2,0,1:T(8,128)} %copy-done.7) | copy-start | bytes 1572868
  128.3 11.6 %copy-start.10 = (f32[16,32,256]{2,0,1:T(8,128)S(1)}, f32[16,32,256]{2,0,1:T(8,128)}, u32[]{:S(2)}) copy-start(f32[16,32,256]{2,0,1:T(8,128)} %copy-done.9) | copy-start | bytes 1572868
  136.6 4.8 %copy-start.13 = (f32[2,16,32,1]{3,1,0,2:T(8,128)}, f32[2,16,32,1]{3,1,0,2:T(8,128)S(1)}, u32[]{:S(2)}) copy-start(f32[2,16,32,1]{3,1,0,2:T(8,128)S(1)} %collective-permute-done.4) | copy-start | bytes 12292
  141.5 1.0 copy-start.12
  142.4 86.2 %collective-permute-start.7 = (f32[2,16,1,256]{3,1,0,2:T(8,128)S(1)}, f32[2,16,1,256]{3,1,0,2:T(8,128)S(1)}, u32[]{:S(2)}, u32[]{:S(2)}) collective-permute-start(f32[2,16,1,256]{3,1,0,2:T(8,128)S(1)} %slice.118), channel_id=1, source_target_pairs={{0,1},{1,2},{2,3},{3,4},{4,5},{5,6},{6,7},{7,8},{8,9},{9,10},{10,1... | collective-permute-start | bytes 98312 | tf_op jit(solution)/shard_map/ppermute | solution.py:18
  212.9 15.7 %collective-permute-start.5 = (f32[2,16,32,1]{3,1,0,2:T(8,128)}, f32[2,16,32,1]{3,1,0,2:T(8,128)}, u32[]{:S(2)}, u32[]{:S(2)}) collective-permute-start(f32[2,16,32,1]{3,1,0,2:T(8,128)} %slice.114), channel_id=1, source_target_pairs={{0,48},{48,96},{96,144},{144,192},{192,240},{240,288},{288,336},{3... | collective-permute-start | bytes 12296 | tf_op jit(solution)/shard_map/ppermute | solution.py:12
where the time goes:
time: 236 us; the launch traced here: 234 us
  blocking collectives  127 us (54%)
  waiting for transfers between devices  37.8 us (16%)
  starting transfers between devices  28.8 us (12%)
  local copies, waits for them, and re-layouts  21.6 us (9%)
  other arithmetic  18.3 us (8%)
    all_gather x2, blocking collectives, per_device(): lax.all_gather(top_terms, 'lon', axis=1, tiled=True)  127 us
    ppermute x4, waiting for transfers between devices, shifted(): return lax.ppermute(value, axis, pairs)  31.6 us
    ppermute x4, starting transfers between devices, passed_along(): return lax.ppermute(array, axis, pairs)  14.8 us
    ppermute x4, starting transfers between devices, shifted(): return lax.ppermute(value, axis, pairs)  14 us
    ppermute x4, waiting for transfers between devices, passed_along(): return lax.ppermute(array, axis, pairs)  6.26 us
    mul x2, other arithmetic, per_device(): masked = cell_open * tracer  5.52 us
  transfers between devices with their start and end apart: 8, of which 5 were waited for; matrix products, arithmetic and copies ran while one was open for 9% of the time, Pallas kernels for 0%

commit v1 on v0

v1 whole, which is shorter than its diff:
```python
import functools

import jax
import jax.numpy as jnp
from jax import lax
from jax.experimental import pallas as pl
from jax.experimental.pallas import tpu as pltpu
from jax.sharding import PartitionSpec as P

LANES = 128
PAD = 8
UNROLL = 4


def loop_levels(levels, body):
    def trip(i, carry):
        for j in range(UNROLL):
            body(i * UNROLL + j)
        return carry

    lax.fori_loop(0, levels // UNROLL, trip, 0)


def kernel(
    n_lon, n_lat,
    ct, u_hbm, v_hbm, d_hbm, w_hbm, cm_hbm, em_hbm, nm_hbm, fp_hbm,
    out,
    a0, a1, nmb, ub, vb, db, wb, cmb, emb, nkb, fps,
    east_c, west_c, north_c, diag_c, down_c,
    send_e, send_w, recv_w, recv_e,
    fq, fg, fx, fy, fo, fb,
    load_sem, send_sem, recv_sem, fold_send, fold_recv,
):
    _, levels, rows, cols = ct.shape
    lon, lat = lax.axis_index("lon"), lax.axis_index("lat")
    east, west = lax.rem(lon + 1, n_lon), lax.rem(lon + n_lon - 1, n_lon)
    is_top, is_bottom = lat == n_lat - 1, lat == 0
    row_tiles = rows // 8
    first, last = PAD, PAD + rows - 1

    barrier = pltpu.get_barrier_semaphore()

    def greet(at):
        pl.semaphore_signal(barrier, inc=1, device_id=at, device_id_type=pl.DeviceIdType.MESH)

    @pl.when(is_top)
    def _():
        def one(p, carry):
            @pl.when(p != lon)
            def _():
                greet((p, lat))
            return carry
        lax.fori_loop(0, n_lon, one, 0)

    @pl.when(jnp.logical_not(is_top))
    def _():
        greet((east, lat))
        greet((west, lat))
        greet((lon, lat + 1))

    @pl.when(jnp.logical_not(is_bottom))
    def _():
        greet((lon, lat - 1))

    loads = []

    def load(src, dst):
        copy = pltpu.make_async_copy(src, dst, load_sem.at[len(loads)])
        copy.start()
        loads.append(copy)
        return copy

    ct_loads = [
        load(
            ct.at[:, :, :, pl.ds(LANES * l, LANES)],
            a0.at[:, pl.ds(1, levels), l, pl.ds(PAD, rows), :],
        )
        for l in range(2)
    ]
    coef_loads = [
        load(cm_hbm, cmb), load(nm_hbm, nkb), load(em_hbm, emb),
        load(d_hbm, db), load(v_hbm, vb), load(u_hbm, ub), load(w_hbm, wb), load(fp_hbm, fps),
    ]

    zeros = jnp.zeros((rows, LANES), jnp.float32)
    for buf in (a0, a1):
        for t in range(2):
            for k in (0, levels + 1):
                for l in range(2):
                    buf[t, k, l, pl.ds(PAD, rows), :] = zeros
    for l in range(2):
        down_c[0, :, LANES * l : LANES * (l + 1)] = zeros

    line = jnp.zeros((1, LANES), jnp.float32)

    @pl.when(is_bottom)
    def _():
        for k in range(levels):
            for l in range(2):
                nmb[k, l, pl.ds(first - 1, 1), :] = line
                for t in range(2):
                    a0[t, k + 1, l, pl.ds(first - 1, 1), :] = line
                    a1[t, k + 1, l, pl.ds(first - 1, 1), :] = line

    @pl.when(is_top)
    def _():
        for k in range(levels):
            for l in range(2):
                for t in range(2):
                    a0[t, k + 1, l, pl.ds(last + 1, 1), :] = line
                    a1[t, k + 1, l, pl.ds(last + 1, 1), :] = line

    lane = lax.broadcasted_iota(jnp.int32, (8, LANES), 1)
    at_first, at_last = lane == 0, lane == LANES - 1

    def moved(value, by):
        return pltpu.roll(value, by, 1)

    def pack_columns(src, dst, l, from_lane):
        def trip(i, acc):
            acc = list(acc)
            for j in range(UNROLL):
                k = i * UNROLL + j
                for t in range(2):
                    q = t * levels + k
                    for r in range(row_tiles):
                        value = src[t, k + 1, l, pl.ds(PAD + 8 * r, 8), :]
                        acc[r] = jnp.where(lane == q, moved(value, lax.rem(q + LANES - from_lane, LANES)), acc[r])
            return tuple(acc)

        acc = lax.fori_loop(
            0, levels // UNROLL, trip, tuple(jnp.zeros((8, LANES), jnp.float32) for _ in range(row_tiles))
        )
        for r in range(row_tiles):
            dst[pl.ds(8 * r, 8), :] = acc[r]

    for copy in ct_loads:
        copy.wait()
    pack_columns(a0, send_w.at[0], 0, 0)
    pack_columns(a0, send_e.at[0], 1, LANES - 1)
    for copy in coef_loads:
        copy.wait()

    zero = jnp.zeros((8, LANES), jnp.float32)

    def coefficients(k):
        bit = jnp.left_shift(jnp.int32(1), k)
        for r in range(row_tiles):
            rr = pl.ds(8 * r, 8)
            faces = []
            for l in range(2):
                cc = slice(LANES * l, LANES * (l + 1))
                half, diff = 0.5 * ub[k, rr, cc], db[k, rr, cc]
                open_e = jnp.bitwise_and(emb[rr, cc], bit) != 0
                plus = jnp.where(open_e, half + diff, 0.0)
                faces.append(jnp.where(open_e, half - diff, 0.0))
                east_c[k, rr, cc] = plus
                half = 0.5 * vb[k, rr, cc]
                open_n = jnp.bitwise_and(nkb[rr, cc], bit) != 0
                north = jnp.where(open_n, half + diff, 0.0)
                north_c[k, rr, cc] = north
                nmb[k, l, pl.ds(PAD + 8 * r, 8), :] = jnp.where(open_n, half - diff, 0.0)
                cells = cmb[rr, cc]
                both = jnp.left_shift(jnp.int32(3), k)
                down = jnp.where(jnp.bitwise_and(cells, both) == both, wb[k, rr, cc], 0.0)
                down_c[k + 1, rr, cc] = down
                here = jnp.where(jnp.bitwise_and(cells, bit) != 0, 1.0, 0.0)
                diag_c[k, rr, cc] = here - plus - north - down - down_c[k, rr, cc]
            turned = [moved(face, 1) for face in faces]
            west_c[k, rr, 0:LANES] = jnp.where(at_first, 0.0, turned[0])
            west_c[k, rr, LANES:cols] = jnp.where(at_first, turned[0], turned[1])
            to = 2 * levels + k
            send_e[0, rr, :] = jnp.where(
                lane == to, moved(faces[1], lax.rem(to + 1, LANES)), send_e[0, rr, :]
            )

    loop_levels(levels, coefficients)

    count = 2 + jnp.where(is_top, n_lon - 3, 1) + jnp.where(is_bottom, 0, 1)
    pl.semaphore_wait(barrier, count)

    def remote(src, dst, sem, at):
        return pltpu.make_async_remote_copy(
            src_ref=src, dst_ref=dst, send_sem=send_sem.at[sem], recv_sem=recv_sem.at[sem],
            device_id=at, device_id_type=pl.DeviceIdType.MESH,
        )

    def exchange(step, buf):
        base = 4 * step
        span = pl.ds(1, levels)
        to_east = remote(send_e.at[step], recv_w.at[step], base, (east, lat))
        to_west = remote(send_w.at[step], recv_e.at[step], base + 1, (west, lat))
        to_north = remote(
            buf.at[:, span, :, last, :], buf.at[:, span, :, first - 1, :], base + 2, (lon, lat + 1)
        )
        to_south = remote(
            buf.at[:, span, :, first, :], buf.at[:, span, :, last + 1, :], base + 3, (lon, lat - 1)
        )
        return to_east, to_west, to_north, to_south

    faces_north = remote(nmb.at[:, :, last, :], nmb.at[:, :, first - 1, :], 8, (lon, lat + 1))

    def start_exchange(copies):
        copies[0].start()
        copies[1].start()

        @pl.when(jnp.logical_not(is_top))
        def _():
            copies[2].start()

        @pl.when(jnp.logical_not(is_bottom))
        def _():
            copies[3].start()

    def wait_recv(copies):
        copies[0].wait_recv()
        copies[1].wait_recv()

        @pl.when(jnp.logical_not(is_bottom))
        def _():
            copies[2].wait_recv()

        @pl.when(jnp.logical_not(is_top))
        def _():
            copies[3].wait_recv()

    def wait_send(copies):
        copies[0].wait_send()
        copies[1].wait_send()

        @pl.when(jnp.logical_not(is_top))
        def _():
            copies[2].wait_send()

        @pl.when(jnp.logical_not(is_bottom))
        def _():
            copies[3].wait_send()

    def fold_copy(src, dst, sem, at):
        return pltpu.make_async_remote_copy(
            src_ref=src, dst_ref=dst, send_sem=fold_send.at[sem], recv_sem=fold_recv.at[sem],
            device_id=(at, lat), device_id_type=pl.DeviceIdType.MESH,
        )

    def others(body):
        def one(i, carry):
            body(lax.rem(lon + i, n_lon))
            return carry
        lax.fori_loop(1, n_lon, one, 0)

    def fold_start(step, buf):
        def products(k, carry):
            for l in range(2):
                face = nmb[k, l, pl.ds(last, 1), :]
                for t in range(2):
                    fq[step, k, pl.ds(2 * t + l, 1), :] = -(face * buf[t, k + 1, l, pl.ds(last, 1), :])
            return carry
        lax.fori_loop(0, levels, products, 0)
        others(lambda p: fold_copy(fq.at[step, p], fg.at[step, lon], 2 * step, p).start())
        fg[step, lon] = fq[step, lon]

    def fold_turn(step):
        some = pl.ds(0, n_lon - 1)
        fold_copy(fq.at[step, some], fg.at[step, some], 2 * step, east).wait_recv()
        fixed = lax.rem(fps[0] + lon * cols, n_lon * cols)
        tile = fixed // LANES
        block, odd = tile // 2, lax.rem(tile, 2)
        within = lax.rem(fixed, LANES)
        source = jnp.bitwise_and(within - lane, LANES - 1)
        low = lane <= within
        keep = jnp.logical_xor(low, jnp.broadcast_to(odd, lane.shape) == 1)
        row = lax.broadcasted_iota(jnp.int32, (8, LANES), 0)
        even_row = jnp.bitwise_and(row, 1) == 0
        for j in range(n_lon):
            turned = jnp.take_along_axis(fg[step, j], source, axis=1, mode="promise_in_bounds")
            fx[j] = turned
            fy[j] = jnp.where(even_row, pltpu.roll(turned, 7, 0), pltpu.roll(turned, 1, 0))
        for i in range(n_lon):
            here = lax.rem(block + n_lon - i, n_lon)
            before = lax.rem(block + 2 * n_lon - i - 1, n_lon)
            swapped = lax.rem(block + 2 * n_lon - i - 1 + odd, n_lon)
            straight = jnp.where(even_row, fx[here], fx[before])
            fo[step, i] = jnp.where(keep, straight, fy[swapped])
        others(lambda p: fold_copy(fo.at[step, p], fb.at[step, lon], 2 * step + 1, p).start())
        fb[step, lon] = fo[step, lon]

    def fold_wait(step):
        some = pl.ds(0, n_lon - 1)
        fold_copy(fo.at[step, some], fb.at[step, some], 2 * step + 1, east).wait_recv()

    def fold_wait_send(step):
        some = pl.ds(0, n_lon - 1)
        fold_copy(fq.at[step, some], fg.at[step, some], 2 * step, east).wait_send()
        fold_copy(fo.at[step, some], fb.at[step, some], 2 * step + 1, east).wait_send()

    def stencil(step, buf, store):
        def level(k):
            for r in range(row_tiles):
                rr = pl.ds(8 * r, 8)
                here = pl.ds(PAD + 8 * r, 8)
                above = pl.ds(PAD + 8 * r + 1, 8)
                below = pl.ds(PAD + 8 * r - 1, 8)
                packed_w, packed_e = recv_w[step, rr, :], recv_e[step, rr, :]
                value = [[buf[t, k + 1, l, here, :] for l in range(2)] for t in range(2)]
                next_e, next_w = [], []
                for t in range(2):
                    q = t * levels + k
                    left = [moved(x, LANES - 1) for x in value[t]]
                    right = [moved(x, 1) for x in value[t]]
                    edge_w = moved(packed_w, lax.rem(LANES - q, LANES))
                    edge_e = moved(packed_e, LANES - 1 - q)
                    next_e.append([jnp.where(at_last, left[1], left[0]), jnp.where(at_last, edge_e, left[1])])
                    next_w.append([jnp.where(at_first, edge_w, right[0]), jnp.where(at_first, right[0], right[1])])
                for l in range(2):
                    cc = slice(LANES * l, LANES * (l + 1))
                    ce, cw, cn = east_c[k, rr, cc], west_c[k, rr, cc], north_c[k, rr, cc]
                    cs = nmb[k, l, below, :]
                    cd, cu, cx = down_c[k + 1, rr, cc], down_c[k, rr, cc], diag_c[k, rr, cc]
                    if step == 0:
                        if l == 0:
                            cw = jnp.where(at_first, moved(packed_w, LANES - 2 * levels - k), cw)
                            west_c[k, rr, cc] = cw
                        cx = cx + cw + cs
                        diag_c[k, rr, cc] = cx
                    for t in range(2):
                        total = (
                            cx * value[t][l]
                            + ce * next_e[t][l]
                            - cw * next_w[t][l]
                            + cn * buf[t, k + 1, l, above, :]
                            - cs * buf[t, k + 1, l, below, :]
                            + cd * buf[t, k + 2, l, here, :]
                            + cu * buf[t, k, l, here, :]
                        )
                        store(t, k, l, r, total)

        loop_levels(levels, level)

    def store_inner(t, k, l, r, total):
        a1[t, k + 1, l, pl.ds(PAD + 8 * r, 8), :] = total

    def store_out(t, k, l, r, total):
        out[t, k, pl.ds(8 * r, 8), LANES * l : LANES * (l + 1)] = total

    copies = exchange(0, a0)
    start_exchange(copies)

    @pl.when(jnp.logical_not(is_top))
    def _():
        faces_north.start()

    @pl.when(is_top)
    def _():
        fold_start(0, a0)

    wait_recv(copies)

    @pl.when(jnp.logical_not(is_bottom))
    def _():
        faces_north.wait_recv()

    @pl.when(is_top)
    def _():
        fold_turn(0)

    stencil(0, a0, store_inner)

    @pl.when(is_top)
    def _():
        fold_wait(0)

        def add(k, carry):
            for t in range(2):
                for l in range(2):
                    at = pl.ds(last, 1)
                    a1[t, k + 1, l, at, :] = a1[t, k + 1, l, at, :] + fb[0, k, pl.ds(2 * t + l, 1), :]
            return carry
        lax.fori_loop(0, levels, add, 0)

    later = exchange(1, a1)

    @pl.when(is_top)
    def _():
        fold_start(1, a1)

    pack_columns(a1, send_w.at[1], 0, 0)
    pack_columns(a1, send_e.at[1], 1, LANES - 1)
    start_exchange(later)

    @pl.when(is_top)
    def _():
        fold_turn(1)

    wait_recv(later)
    stencil(1, a1, store_out)

    @pl.when(is_top)
    def _():
        fold_wait(1)

        def add(k, carry):
            for t in range(2):
                for l in range(2):
                    cc = slice(LANES * l, LANES * (l + 1))
                    at = pl.ds(rows - 1, 1)
                    out[t, k, at, cc] = out[t, k, at, cc] + fb[1, k, pl.ds(2 * t + l, 1), :]
            return carry
        lax.fori_loop(0, levels, add, 0)

    wait_send(copies)
    wait_send(later)

    @pl.when(jnp.logical_not(is_top))
    def _():
        faces_north.wait_send()

    @pl.when(is_top)
    def _():
        fold_wait_send(0)
        fold_wait_send(1)


def per_device(n_lon, n_lat, *args):
    _, levels, rows, cols = args[0].shape
    f32, i32 = jnp.float32, jnp.int32
    field = (levels, rows, cols)
    padded = (2, levels + 2, 2, rows + 2 * PAD, LANES)
    return pl.pallas_call(
        functools.partial(kernel, n_lon, n_lat),
        out_shape=jax.ShapeDtypeStruct(args[0].shape, f32),
        in_specs=[pl.BlockSpec(memory_space=pltpu.HBM)] * 9,
        out_specs=pl.BlockSpec(memory_space=pltpu.VMEM),
        scratch_shapes=[
            pltpu.VMEM(padded, f32),
            pltpu.VMEM(padded, f32),
            pltpu.VMEM((levels, 2, rows + 2 * PAD, LANES), f32),
            *[pltpu.VMEM(field, f32) for _ in range(4)],
            *[pltpu.VMEM((rows, cols), i32) for _ in range(3)],
            pltpu.SMEM((cols,), i32),
            *[pltpu.VMEM(field, f32) for _ in range(4)],
            pltpu.VMEM((levels + 1, rows, cols), f32),
            *[pltpu.VMEM((2, rows, LANES), f32) for _ in range(4)],
            pltpu.VMEM((2, levels, 8, LANES), f32),
            pltpu.VMEM((2, n_lon, 8, LANES), f32),
            pltpu.VMEM((n_lon, 8, LANES), f32),
            pltpu.VMEM((n_lon, 8, LANES), f32),
            pltpu.VMEM((2, n_lon, 8, LANES), f32),
            pltpu.VMEM((2, levels, 8, LANES), f32),
            pltpu.SemaphoreType.DMA((10,)),
            pltpu.SemaphoreType.DMA((9,)),
            pltpu.SemaphoreType.DMA((9,)),
            pltpu.SemaphoreType.DMA((4,)),
            pltpu.SemaphoreType.DMA((4,)),
        ],
        compiler_params=pltpu.CompilerParams(
            collective_id=0, has_side_effects=True, vmem_limit_bytes=32 * 1024 * 1024
        ),
    )(*args)


def solution(mesh):
    n_lon, n_lat = mesh.shape["lon"], mesh.shape["lat"]
    placed = (
        P(None, None, "lat", "lon"),
        P(None, "lat", "lon"),
        P(None, "lat", "lon"),
        P(None, "lat", "lon"),
        P(None, "lat", "lon"),
        P("lat", "lon"),
        P("lat", "lon"),
        P("lat", "lon"),
        P("lon"),
    )
    return jax.shard_map(
        functools.partial(per_device, n_lon, n_lat),
        mesh=mesh,
        in_specs=placed,
        out_specs=P(None, None, "lat", "lon"),
        check_vma=False,
    )
```

time: 236 us -> 34.4 us (0.15)
  blocking collectives: 127 us -> 0 us
  waiting for transfers between devices: 37.8 us -> 0 us
  starting transfers between devices: 28.8 us -> 0 us
  Pallas kernels: 0 us -> 24.5 us
  other arithmetic: 18.3 us -> 0 us
  local copies, waits for them, and re-layouts: 21.6 us -> 9.31 us
    all_gather x2 -> x0, blocking collectives: 127 us -> none  [per_device(): lax.all_gather(top_terms, 'lon', axis=1, tiled=True)]
    ppermute x8 -> x0, waiting for transfers between devices: 37.8 us -> none  [the longest x4 31.6 us: shifted(): return lax.ppermute(value, axis, pairs)]
    ppermute x8 -> x0, starting transfers between devices: 28.8 us -> none  [the longest x4 14.8 us: passed_along(): return lax.ppermute(array, axis, pairs)]
    pallas_call x0 -> x1, Pallas kernels: none -> 24.5 us  [per_device(): pl.pallas_call(functools.partial(kernel, n_lon, n_lat), out_shape=jax.Sha...]
    mul x8 -> x0, other arithmetic: 13.1 us -> none  [the longest x2 5.52 us: per_device(): masked = cell_open * tracer]
    slice x14 -> x0, local copies, waits for them, and re-layouts: 9.4 us -> none  [the longest x2 4.61 us: per_device(): north_push[:, :, :-1, :]]
    unnamed x38 -> x19, local copies, waits for them, and re-layouts: 2.22 us -> 9.31 us
    gather x2 -> x0, local copies, waits for them, and re-layouts: 4.63 us -> none  [select_partner(): picked = jnp.take(piece_rows, jnp.clip(partner_cols, 0, width - 1), axis=1)]
  transfers between devices with their start and end apart: 8 -> 0, of which waited for: 5 -> 0; matrix products, arithmetic and copies ran while one was open for 9% -> 0% of each run, Pallas kernels for 0% -> 0%
where the time goes in v1:
time: 34.4 us; the launch traced here: 33.8 us
  Pallas kernels  24.5 us (71%)
  local copies, waits for them, and re-layouts  9.31 us (27%)
    pallas_call x1, Pallas kernels, per_device(): pl.pallas_call(functools.partial(kernel, n_lon, n_lat), out_shape=jax.Sha...  24.5 us
    unnamed x19, local copies, waits for them, and re-layouts  9.31 us

profile of v1, /device:TPU:1, one launch (start us, length us, event | category | flops | bytes accessed | tf_op | source)
XLA Modules:
  0.0 33.8 jit_solution(18077055950989386114)
XLA Ops:
  0.0 0.0 copy-start
  0.0 1.2 %copy-done = f32[2,16,32,256]{3,2,1,0:T(8,128)S(1)} copy-done((f32[2,16,32,256]{3,2,1,0:T(8,128)S(1)}, f32[2,16,32,256]{3,2,1,0:T(8,128)}, u32[]{:S(2)}) %copy-start) | copy-done | bytes 1048600
  1.2 0.0 copy-start.1
  1.2 1.0 %copy-done.1 = f32[16,32,256]{2,1,0:T(8,128)S(1)} copy-done((f32[16,32,256]{2,1,0:T(8,128)S(1)}, f32[16,32,256]{2,1,0:T(8,128)}, u32[]{:S(2)}) %copy-start.1) | copy-done | bytes 524312
  2.3 0.0 copy-start.2
  2.3 1.0 %copy-done.2 = f32[16,32,256]{2,1,0:T(8,128)S(1)} copy-done((f32[16,32,256]{2,1,0:T(8,128)S(1)}, f32[16,32,256]{2,1,0:T(8,128)}, u32[]{:S(2)}) %copy-start.2) | copy-done | bytes 524312
  3.3 0.0 copy-start.3
  3.3 1.0 %copy-done.3 = f32[16,32,256]{2,1,0:T(8,128)S(1)} copy-done((f32[16,32,256]{2,1,0:T(8,128)S(1)}, f32[16,32,256]{2,1,0:T(8,128)}, u32[]{:S(2)}) %copy-start.3) | copy-done | bytes 524312
  4.4 0.0 copy-start.4
  4.4 1.0 %copy-done.4 = f32[16,32,256]{2,1,0:T(8,128)S(1)} copy-done((f32[16,32,256]{2,1,0:T(8,128)S(1)}, f32[16,32,256]{2,1,0:T(8,128)}, u32[]{:S(2)}) %copy-start.4) | copy-done | bytes 524312
  5.4 0.0 copy-start.5
  5.4 0.8 %copy-done.5 = s32[32,256]{1,0:T(8,128)S(1)} copy-done((s32[32,256]{1,0:T(8,128)S(1)}, s32[32,256]{1,0:T(8,128)}, u32[]{:S(2)}) %copy-start.5) | copy-done | bytes 32792
  6.2 0.0 copy-start.6
  6.2 0.8 %copy-done.6 = s32[32,256]{1,0:T(8,128)S(1)} copy-done((s32[32,256]{1,0:T(8,128)S(1)}, s32[32,256]{1,0:T(8,128)}, u32[]{:S(2)}) %copy-start.6) | copy-done | bytes 32792
  6.9 0.0 copy-start.7
  6.9 0.8 %copy-done.7 = s32[32,256]{1,0:T(8,128)S(1)} copy-done((s32[32,256]{1,0:T(8,128)S(1)}, s32[32,256]{1,0:T(8,128)}, u32[]{:S(2)}) %copy-start.7) | copy-done | bytes 32792
  7.7 0.0 copy-start.8
  7.7 0.7 %copy-done.8 = s32[256]{0:T(256)S(1)} copy-done((s32[256]{0:T(256)S(1)}, s32[256]{0:T(256)}, u32[]{:S(2)}) %copy-start.8) | copy-done | bytes 1048
  8.3 24.5 %shard_map.91 = f32[2,16,32,256]{3,2,1,0:T(8,128)S(1)} custom-call(f32[2,16,32,256]{3,2,1,0:T(8,128)S(1)} %copy-done, f32[16,32,256]{2,1,0:T(8,128)S(1)} %copy-done.1, f32[16,32,256]{2,1,0:T(8,128)S(1)} %copy-done.2, f32[16,32,256]{2,1,0:T(8,128)S(1)} %copy-done.3, f32[16,32,256]{2,1,0:T(8,128)S(1)} %copy-done.4, s32[32,256]{1,0:T(8,128)S(1)} %copy-done.5, ...), custom_call_target="tpu_custom_call" | custom-call | tf_op jit(solution)/shard_map/pallas_call | solution.py:428
  32.8 1.0 %copy.11 = f32[2,16,32,256]{3,2,1,0:T(8,128)} copy(f32[2,16,32,256]{3,2,1,0:T(8,128)S(1)} %shard_map.91) | data formatting | bytes 2097152
Async XLA Ops:
  0.0 1.2 %copy-start = (f32[2,16,32,256]{3,2,1,0:T(8,128)S(1)}, f32[2,16,32,256]{3,2,1,0:T(8,128)}, u32[]{:S(2)}) copy-start(f32[2,16,32,256]{3,2,1,0:T(8,128)} %ct.1) | copy-start | bytes 3145732
  1.2 1.0 %copy-start.1 = (f32[16,32,256]{2,1,0:T(8,128)S(1)}, f32[16,32,256]{2,1,0:T(8,128)}, u32[]{:S(2)}) copy-start(f32[16,32,256]{2,1,0:T(8,128)} %u_hbm.1) | copy-start | bytes 1572868
  2.3 1.0 %copy-start.2 = (f32[16,32,256]{2,1,0:T(8,128)S(1)}, f32[16,32,256]{2,1,0:T(8,128)}, u32[]{:S(2)}) copy-start(f32[16,32,256]{2,1,0:T(8,128)} %v_hbm.1) | copy-start | bytes 1572868
  3.3 1.0 %copy-start.3 = (f32[16,32,256]{2,1,0:T(8,128)S(1)}, f32[16,32,256]{2,1,0:T(8,128)}, u32[]{:S(2)}) copy-start(f32[16,32,256]{2,1,0:T(8,128)} %d_hbm.1) | copy-start | bytes 1572868
  4.4 1.0 %copy-start.4 = (f32[16,32,256]{2,1,0:T(8,128)S(1)}, f32[16,32,256]{2,1,0:T(8,128)}, u32[]{:S(2)}) copy-start(f32[16,32,256]{2,1,0:T(8,128)} %w_hbm.1) | copy-start | bytes 1572868
  5.4 0.8 %copy-start.5 = (s32[32,256]{1,0:T(8,128)S(1)}, s32[32,256]{1,0:T(8,128)}, u32[]{:S(2)}) copy-start(s32[32,256]{1,0:T(8,128)} %cm_hbm.1) | copy-start | bytes 98308
  6.2 0.8 %copy-start.6 = (s32[32,256]{1,0:T(8,128)S(1)}, s32[32,256]{1,0:T(8,128)}, u32[]{:S(2)}) copy-start(s32[32,256]{1,0:T(8,128)} %em_hbm.1) | copy-start | bytes 98308
  6.9 0.8 %copy-start.7 = (s32[32,256]{1,0:T(8,128)S(1)}, s32[32,256]{1,0:T(8,128)}, u32[]{:S(2)}) copy-start(s32[32,256]{1,0:T(8,128)} %nm_hbm.1) | copy-start | bytes 98308
  7.7 0.7 %copy-start.8 = (s32[256]{0:T(256)S(1)}, s32[256]{0:T(256)}, u32[]{:S(2)}) copy-start(s32[256]{0:T(256)} %fp_hbm.1) | copy-start | bytes 3076

commit v2 on v0

v2 whole, which is shorter than its diff:
```python
import functools

import jax
import jax.numpy as jnp
from jax import lax
from jax.experimental import pallas as pl
from jax.experimental.pallas import tpu as pltpu
from jax.sharding import PartitionSpec as P

LANES = 128
PAD = 8
CHUNK = 4
MESH = pl.DeviceIdType.MESH


def kernel(
    n_lon, n_lat,
    ct, u_hbm, v_hbm, d_hbm, w_hbm, cm_hbm, em_hbm, nm_hbm, fp_hbm,
    out,
    a0, a1, nmb, ub, vb, db, wb, cmb, emb, nkb, fps,
    ctr, ur, vr, dr, wr,
    east_c, west_c, north_c, diag_c, down_c,
    row_n, row_s, from_s, from_n,
    col_e, col_w, from_w, from_e, next_e, next_w, next_from_w, next_from_e,
    c_sw, c_se, c_nw, c_ne,
    edge, add_w, add_e,
    fg, fq, fx, fy, f1, f2, fo, fb,
    load_sem, send_sem, recv_sem, fold_send, fold_recv,
):
    _, levels, rows, cols = ct.shape
    lon, lat = lax.axis_index("lon"), lax.axis_index("lat")
    east, west = lax.rem(lon + 1, n_lon), lax.rem(lon + n_lon - 1, n_lon)
    is_top, is_bottom = lat == n_lat - 1, lat == 0
    has_north, has_south = jnp.logical_not(is_top), jnp.logical_not(is_bottom)
    tiles = rows // 8
    first, last = PAD, PAD + rows - 1
    both = 2 * levels
    chunks = levels // CHUNK

    barrier = pltpu.get_barrier_semaphore()

    def greet(at):
        pl.semaphore_signal(barrier, inc=1, device_id=at, device_id_type=MESH)

    def others(body):
        def one(i, carry):
            body(lax.rem(lon + i, n_lon))
            return carry

        lax.fori_loop(1, n_lon, one, 0)

    @pl.when(is_top)
    def _():
        others(lambda p: greet((p, lat)))

    @pl.when(has_north)
    def _():
        greet((east, lat))
        greet((west, lat))
        greet((east, lat + 1))
        greet((west, lat + 1))
        greet((lon, lat + 1))

    @pl.when(has_south)
    def _():
        greet((east, lat - 1))
        greet((west, lat - 1))
        greet((lon, lat - 1))

    def load(src, dst, sem):
        copy = pltpu.make_async_copy(src, dst, load_sem.at[sem])
        copy.start()
        return copy

    tops = (0, 1, rows - 2, rows - 1)
    row_loads = [load(cm_hbm, cmb, 0), load(em_hbm, emb, 1), load(nm_hbm, nkb, 2)]
    for i, row in enumerate(tops):
        row_loads.append(load(ct.at[:, :, row, :], ctr.at[i], 3 + i))
    for i, row in enumerate((0, rows - 1)):
        row_loads.append(load(u_hbm.at[:, row, :], ur.at[i], 7 + i))
        row_loads.append(load(w_hbm.at[:, row, :], wr.at[i], 9 + i))
    for i, row in enumerate((0, rows - 2, rows - 1)):
        row_loads.append(load(v_hbm.at[:, row, :], vr.at[i], 11 + i))
        row_loads.append(load(d_hbm.at[:, row, :], dr.at[i], 14 + i))
    fold_load = load(fp_hbm, fps, 17)

    def chunk_loads(c):
        span = pl.ds(CHUNK * c, CHUNK)
        base = 18 + 6 * c
        pairs = [
            (
                ct.at[:, span, :, pl.ds(LANES * l, LANES)],
                a0.at[:, pl.ds(CHUNK * c + 1, CHUNK), l, pl.ds(PAD, rows), :],
            )
            for l in range(2)
        ]
        pairs += [(src.at[span], dst.at[span]) for src, dst in ((u_hbm, ub), (d_hbm, db), (v_hbm, vb), (w_hbm, wb))]
        return [pltpu.make_async_copy(src, dst, load_sem.at[base + i]) for i, (src, dst) in enumerate(pairs)]

    for c in range(chunks):
        for copy in chunk_loads(c):
            copy.start()

    block = jnp.zeros((rows, LANES), jnp.float32)
    line = jnp.zeros((1, LANES), jnp.float32)
    for buf in (a0, a1):
        for t in range(2):
            for k in (0, levels + 1):
                for l in range(2):
                    buf[t, k, l, pl.ds(PAD, rows), :] = block
    for l in range(2):
        down_c[0, :, LANES * l : LANES * (l + 1)] = block

    def clear(k, carry):
        for l in range(2):
            nmb[k, l, pl.ds(first - 1, 1), :] = line
            for t in range(2):
                a0[t, k + 1, l, pl.ds(first - 1, 1), :] = line
                a0[t, k + 1, l, pl.ds(last + 1, 1), :] = line
        return carry

    lax.fori_loop(0, levels, clear, 0)

    @pl.when(is_bottom)
    def _():
        from_s[...] = jnp.zeros_like(from_s)
        c_sw[...] = jnp.zeros_like(c_sw)
        c_se[...] = jnp.zeros_like(c_se)

    @pl.when(is_top)
    def _():
        from_n[...] = jnp.zeros_like(from_n)
        c_nw[...] = jnp.zeros_like(c_nw)
        c_ne[...] = jnp.zeros_like(c_ne)

    lane = lax.broadcasted_iota(jnp.int32, (8, LANES), 1)
    sub = lax.broadcasted_iota(jnp.int32, (8, LANES), 0)
    at_first, at_last = lane == 0, lane == LANES - 1
    row_lane = lax.broadcasted_iota(jnp.int32, (levels, LANES), 1)
    row_level = lax.broadcasted_iota(jnp.int32, (levels, LANES), 0)
    row_first, row_last = row_lane == 0, row_lane == LANES - 1

    def moved(value, by):
        return pltpu.roll(value, by, 1)

    def halves(l):
        return slice(LANES * l, LANES * (l + 1))

    for copy in row_loads:
        copy.wait()

    def bits(buf, row, count=1):
        mask = jnp.left_shift(jnp.full((levels, LANES), 2**count - 1, jnp.int32), row_level)
        return [jnp.bitwise_and(jnp.broadcast_to(buf[pl.ds(row, 1), halves(l)], mask.shape), mask) == mask for l in range(2)]

    def edge_row(i, row):
        at = 3 * i
        cell = [ctr[at, t] for t in range(2)]
        inner = [ctr[1 + i, t] for t in range(2)]
        open_e, open_n, open_c, open_d = bits(emb, row), bits(nkb, row), bits(cmb, row), bits(cmb, row, 2)
        plus, minus, north, south, diag, down = [], [], [], [], [], []
        for l in range(2):
            half, diff = 0.5 * ur[i, :, halves(l)], dr[2 * i, :, halves(l)]
            plus.append(jnp.where(open_e[l], half + diff, 0.0))
            minus.append(jnp.where(open_e[l], half - diff, 0.0))
            half = 0.5 * vr[2 * i, :, halves(l)]
            north.append(jnp.where(open_n[l], half + diff, 0.0))
            south.append(jnp.where(open_n[l], half - diff, 0.0))
            down.append(jnp.where(open_d[l], wr[i, :, halves(l)], 0.0))
        turned = [moved(x, 1) for x in minus]
        side = [jnp.where(row_first, 0.0, turned[0]), jnp.where(row_first, turned[0], turned[1])]
        if i == 1:
            open_b = bits(nkb, row - 1)
            beyond = [jnp.where(open_b[l], 0.5 * vr[1, :, halves(l)] - dr[1, :, halves(l)], 0.0) for l in range(2)]
        result = [[None, None], [None, None]]
        for l in range(2):
            up = pltpu.roll(down[l], 1, 0)
            diag = jnp.where(open_c[l], 1.0, 0.0) - plus[l] - north[l] - down[l] - up + side[l]
            if i == 1:
                diag = diag + beyond[l]
            for t in range(2):
                here = cell[t][:, halves(l)]
                left = [moved(cell[t][:, halves(m)], LANES - 1) for m in range(2)]
                right = [moved(cell[t][:, halves(m)], 1) for m in range(2)]
                to_e = jnp.where(row_last, left[1], left[0]) if l == 0 else jnp.where(row_last, 0.0, left[1])
                to_w = right[0] if l == 0 else jnp.where(row_first, right[0], right[1])
                total = diag * here + plus[l] * to_e - side[l] * to_w
                total = total + down[l] * pltpu.roll(here, levels - 1, 0) + up * pltpu.roll(here, 1, 0)
                if i == 0:
                    total = total + north[l] * inner[t][:, halves(l)]
                else:
                    total = total - beyond[l] * inner[t][:, halves(l)]
                result[t][l] = total
        return cell, result, plus, minus, north, south

    cell, result, plus, minus, north, south = edge_row(1, rows - 1)
    for l in range(2):
        for t in range(2):
            row_n[2 * t + l] = cell[t][:, halves(l)]
            row_n[4 + 2 * t + l] = result[t][l]
        row_n[8 + l] = south[l]
        row_n[10 + l] = north[l]
    row_n[12] = plus[1]
    row_n[13] = minus[1]
    cell, result, plus, minus, north, south = edge_row(0, 0)
    for l in range(2):
        for t in range(2):
            row_s[2 * t + l] = cell[t][:, halves(l)]
            row_s[4 + 2 * t + l] = result[t][l]
    row_s[8] = plus[1]

    count = 2 + jnp.where(is_top, n_lon - 3, 3) + jnp.where(is_bottom, 0, 3)
    pl.semaphore_wait(barrier, count)

    def remote(src, dst, sem, at):
        return pltpu.make_async_remote_copy(
            src_ref=src, dst_ref=dst, send_sem=send_sem.at[sem], recv_sem=recv_sem.at[sem],
            device_id=at, device_id_type=MESH,
        )

    to_north = remote(row_n.at[pl.ds(0, 13)], from_s.at[pl.ds(0, 13)], 0, (lon, lat + 1))
    to_south = remote(row_s, from_n, 1, (lon, lat - 1))
    to_east = remote(col_e, from_w, 2, (east, lat))
    to_west = remote(col_w, from_e, 3, (west, lat))
    later_east = remote(next_e, next_from_w, 4, (east, lat))
    later_west = remote(next_w, next_from_e, 5, (west, lat))
    tail = pl.ds(rows - 8, 8)
    to_ne = remote(col_e.at[tail], c_sw, 6, (east, lat + 1))
    to_nw = remote(col_w.at[tail], c_se, 7, (west, lat + 1))
    to_se = remote(col_e.at[pl.ds(0, 8)], c_nw, 8, (east, lat - 1))
    to_sw = remote(col_w.at[pl.ds(0, 8)], c_ne, 9, (west, lat - 1))

    def fold_copy(src, dst, sem, at):
        return pltpu.make_async_remote_copy(
            src_ref=src, dst_ref=dst, send_sem=fold_send.at[sem], recv_sem=fold_recv.at[sem],
            device_id=(at, lat), device_id_type=MESH,
        )

    some = pl.ds(0, n_lon - 1)
    fold_out = fold_copy(fq.at[some], fg.at[some], 0, east)
    fold_back = fold_copy(fo.at[some], fb.at[some], 1, east)

    @pl.when(has_north)
    def _():
        to_north.start()

    @pl.when(is_top)
    def _():
        def collect(k, carry):
            for i in range(14):
                fq[k, pl.ds(i, 1), :] = row_n[i, pl.ds(k, 1), :]
            return carry

        lax.fori_loop(0, levels, collect, 0)
        others(lambda p: fold_copy(fq.at[p], fg.at[lon], 0, p).start())
        fg[lon] = fq[lon]

    @pl.when(has_south)
    def _():
        to_south.start()

    col_e[...] = jnp.zeros_like(col_e)
    col_w[...] = jnp.zeros_like(col_w)

    def coefficients(c, carry):
        for copy in chunk_loads(c):
            copy.wait()
        for r in range(tiles):
            rr, pr = pl.ds(8 * r, 8), pl.ds(PAD + 8 * r, 8)
            pack_e, pack_w = col_e[rr, :], col_w[rr, :]
            for j in range(CHUNK):
                k = CHUNK * c + j
                bit = jnp.left_shift(jnp.int32(1), k)
                pair = jnp.left_shift(jnp.int32(3), k)
                minus, plus, norths, souths = [], [], [], []
                for l in range(2):
                    cc = halves(l)
                    half, diff = 0.5 * ub[k, rr, cc], db[k, rr, cc]
                    open_e = jnp.bitwise_and(emb[rr, cc], bit) != 0
                    plus.append(jnp.where(open_e, half + diff, 0.0))
                    minus.append(jnp.where(open_e, half - diff, 0.0))
                    half = 0.5 * vb[k, rr, cc]
                    open_n = jnp.bitwise_and(nkb[rr, cc], bit) != 0
                    norths.append(jnp.where(open_n, half + diff, 0.0))
                    souths.append(jnp.where(open_n, half - diff, 0.0))
                turned = [moved(x, 1) for x in minus]
                side = [jnp.where(at_first, 0.0, turned[0]), jnp.where(at_first, turned[0], turned[1])]
                for l in range(2):
                    cc = halves(l)
                    cells = cmb[rr, cc]
                    down = jnp.where(jnp.bitwise_and(cells, pair) == pair, wb[k, rr, cc], 0.0)
                    east_c[k, rr, cc] = plus[l]
                    west_c[k, rr, cc] = side[l]
                    north_c[k, rr, cc] = norths[l]
                    nmb[k, l, pr, :] = souths[l]
                    down_c[k + 1, rr, cc] = down
                    here = jnp.where(jnp.bitwise_and(cells, bit) != 0, 1.0, 0.0)
                    below = nmb[k, l, pl.ds(PAD + 8 * r - 1, 8), :]
                    diag_c[k, rr, cc] = here - plus[l] - norths[l] - down - down_c[k, rr, cc] + side[l] + below

                def put(pack, value, lane_to, lane_from):
                    return jnp.where(lane == lane_to, moved(value, lax.rem(lane_to + LANES - lane_from, LANES)), pack)

                for t in range(2):
                    pack_e = put(pack_e, a0[t, k + 1, 1, pr, :], t * levels + k, LANES - 1)
                    pack_w = put(pack_w, a0[t, k + 1, 0, pr, :], t * levels + k, 0)
                pack_e = put(pack_e, minus[1], both + k, LANES - 1)
                pack_e = put(pack_e, plus[1], 2 * both + k, LANES - 1)
                if r == tiles - 1:
                    pack_e = put(pack_e, souths[1], 3 * both + k, LANES - 1)
                    pack_w = put(pack_w, souths[0], both + k, 0)
                    pack_w = put(pack_w, norths[0], 2 * both + k, 0)
                    extra = pl.ds(rows, 8)
                    col_e[extra, :] = put(col_e[extra, :], norths[1], k, LANES - 1)
            col_e[rr, :] = pack_e
            col_w[rr, :] = pack_w
        return carry

    lax.fori_loop(0, chunks, coefficients, 0)

    def doubled(pack, starts):
        again = moved(pack, levels)
        for start in starts:
            pack = jnp.where(jnp.logical_and(lane >= start + levels, lane < start + both), again, pack)
        return pack

    for r in range(tiles):
        rr = pl.ds(8 * r, 8)
        col_e[rr, :] = doubled(col_e[rr, :], (both, 2 * both, 3 * both))
    extra = pl.ds(rows, 8)
    col_e[extra, :] = doubled(col_e[extra, :], (0,))
    col_w[tail, :] = doubled(col_w[tail, :], (both, 2 * both))

    to_east.start()
    to_west.start()

    @pl.when(has_north)
    def _():
        to_ne.start()
        to_nw.start()

    @pl.when(has_south)
    def _():
        to_se.start()
        to_sw.start()

    def first_step(c, carry):
        for r in range(tiles):
            rr, here = pl.ds(8 * r, 8), pl.ds(PAD + 8 * r, 8)
            above, below = pl.ds(PAD + 8 * r + 1, 8), pl.ds(PAD + 8 * r - 1, 8)
            for j in range(CHUNK):
                k = CHUNK * c + j
                for l in range(2):
                    cc = halves(l)
                    ce, cw, cn, cs = east_c[k, rr, cc], west_c[k, rr, cc], north_c[k, rr, cc], nmb[k, l, below, :]
                    cd, cu, cx = down_c[k + 1, rr, cc], down_c[k, rr, cc], diag_c[k, rr, cc]
                    for t in range(2):
                        value = [a0[t, k + 1, m, here, :] for m in range(2)]
                        left_1 = moved(value[1], LANES - 1)
                        right_0 = moved(value[0], 1)
                        if l == 0:
                            to_e, to_w = jnp.where(at_last, left_1, moved(value[0], LANES - 1)), right_0
                        else:
                            to_e = jnp.where(at_last, 0.0, left_1)
                            to_w = jnp.where(at_first, right_0, moved(value[1], 1))
                        total = (
                            cx * value[l]
                            + ce * to_e
                            - cw * to_w
                            + cn * a0[t, k + 1, l, above, :]
                            - cs * a0[t, k + 1, l, below, :]
                            + cd * a0[t, k + 2, l, here, :]
                            + cu * a0[t, k, l, here, :]
                        )
                        a1[t, k + 1, l, here, :] = total
        return carry

    lax.fori_loop(0, chunks, first_step, 0)

    def pack_result(c, packs):
        packs = list(packs)
        for j in range(CHUNK):
            k = CHUNK * c + j
            for t in range(2):
                q = t * levels + k
                for r in range(tiles):
                    here = pl.ds(PAD + 8 * r, 8)
                    packs[r] = jnp.where(lane == q, moved(a1[t, k + 1, 1, here, :], q + 1), packs[r])
                    packs[tiles + r] = jnp.where(lane == q, moved(a1[t, k + 1, 0, here, :], q), packs[tiles + r])
        return tuple(packs)

    packs = lax.fori_loop(0, chunks, pack_result, tuple(jnp.zeros((8, LANES), jnp.float32) for _ in range(2 * tiles)))
    for r in range(tiles):
        next_e[pl.ds(8 * r, 8), :] = packs[r]
        next_w[pl.ds(8 * r, 8), :] = packs[tiles + r]
    later_east.start()
    later_west.start()

    even = jnp.bitwise_and(sub, 1) == 0

    @pl.when(is_top)
    def _():
        fold_load.wait()
        fold_out.wait_recv()
        fixed = lax.rem(fps[0] + lon * cols, n_lon * cols)
        tile = fixed // LANES
        home, odd = tile // 2, lax.rem(tile, 2)
        within = lax.rem(fixed, LANES)
        source = jnp.bitwise_and(within - lane, LANES - 1)
        keep = jnp.logical_xor(lane <= within, jnp.broadcast_to(odd, lane.shape) == 1)

        def faces(j, at):
            shape = (8, LANES)
            return jnp.where(
                even,
                jnp.broadcast_to(fg[j, pl.ds(at, 1), :], shape),
                jnp.broadcast_to(fg[j, pl.ds(at + 1, 1), :], shape),
            )

        def turn(j, value):
            turned = jnp.take_along_axis(value, source, axis=1, mode="promise_in_bounds")
            fx[j] = turned
            fy[j] = jnp.where(even, pltpu.roll(turned, 7, 0), pltpu.roll(turned, 1, 0))

        def turned(i):
            here = lax.rem(home + n_lon - i, n_lon)
            before = lax.rem(home + 2 * n_lon - i - 1, n_lon)
            swapped = lax.rem(home + 2 * n_lon - i - 1 + odd, n_lon)
            return jnp.where(keep, jnp.where(even, fx[here], fx[before]), fy[swapped])

        for j in range(n_lon):
            turn(j, -(faces(j, 8) * fg[j, pl.ds(0, 8), :]))
        for i in range(n_lon):
            f1[i] = turned(i)
        for j in range(n_lon):
            e, w = (j + 1) % n_lon, (j - 1) % n_lon
            own = fg[j, pl.ds(0, 8), :]
            to_w = pltpu.roll(moved(fg[w, pl.ds(0, 8), :], 1), 7, 0)
            to_e = pltpu.roll(moved(fg[e, pl.ds(0, 8), :], LANES - 1), 1, 0)
            face_w = moved(jnp.broadcast_to(fg[w, pl.ds(13, 1), :], (8, LANES)), 1)
            face_e = jnp.broadcast_to(fg[j, pl.ds(12, 1), :], (8, LANES))
            inner = pltpu.roll(own, 4, 0) + f1[j]
            inner = inner + jnp.where(jnp.logical_and(even, at_first), face_w * (own - to_w), 0.0)
            inner = inner + jnp.where(jnp.logical_and(jnp.logical_not(even), at_last), face_e * to_e, 0.0)
            f2[j] = -(faces(j, 8) * inner)
        for j in range(n_lon):
            turn(j, f2[j])
        low = sub < 4
        for i in range(n_lon):
            e, w = (i + 1) % n_lon, (i - 1) % n_lon
            fo[i, pl.ds(0, 8), :] = jnp.where(low, f1[i], pltpu.roll(turned(i), 4, 0))
            fo[i, pl.ds(8, 8), :] = jnp.where(low, f1[w], pltpu.roll(f1[e], 4, 0))
        others(lambda p: fold_copy(fo.at[p], fb.at[lon], 1, p).start())
        fb[lon] = fo[lon]

    @pl.when(has_south)
    def _():
        to_north.wait_recv()
        to_ne.wait_recv()
        to_nw.wait_recv()

    @pl.when(has_north)
    def _():
        to_south.wait_recv()
        to_se.wait_recv()
        to_sw.wait_recv()

    to_east.wait_recv()
    to_west.wait_recv()
    later_east.wait_recv()
    later_west.wait_recv()

    def upright(ref, row, base):
        spread = jnp.broadcast_to(ref[pl.ds(row, 1), :], (levels, LANES))
        return jnp.sum(jnp.where(row_lane == row_level + base, spread, 0.0), axis=1, keepdims=True)

    face_sw, face_nw = upright(c_sw, 7, both), upright(c_nw, 0, both)
    for t in range(2):
        point = t * levels
        for l in range(2):
            at = 2 * t + l
            own, there = row_s[at], from_s[at]
            edge[at] = from_s[8 + l] * (own - there)
            ghost = from_s[4 + at] + from_s[10 + l] * own
            if l == 0:
                ghost = ghost + jnp.where(row_first, face_sw * (there - upright(c_sw, 7, point)), 0.0)
            else:
                ghost = ghost + jnp.where(row_last, from_s[12] * upright(c_se, 7, point), 0.0)
            edge[8 + at] = ghost
            own, there = row_n[at], from_n[at]
            edge[4 + at] = row_n[10 + l] * there
            ghost = from_n[4 + at] + row_n[8 + l] * (there - own)
            if l == 0:
                ghost = ghost + jnp.where(row_first, face_nw * (there - upright(c_nw, 0, point)), 0.0)
            else:
                ghost = ghost + jnp.where(row_last, from_n[8] * upright(c_ne, 0, point), 0.0)
            edge[12 + at] = jnp.where(is_top, 0.0, ghost)

    for r in range(tiles):
        rr = pl.ds(8 * r, 8)
        got = from_w[rr, :]
        own = col_w[rr, :]
        face = moved(got, LANES - both)
        ghost = next_from_w[rr, :] + moved(got, LANES - 2 * both) * own
        if r == 0:
            corner = c_sw[...]
            beyond = pltpu.roll(moved(corner, LANES - 3 * both), 1, 0)
            ghost = ghost + jnp.where(sub == 0, beyond * (got - pltpu.roll(corner, 1, 0)), 0.0)
        if r == tiles - 1:
            ghost = ghost + jnp.where(sub == 7, from_w[extra, :] * pltpu.roll(c_nw[...], 7, 0), 0.0)
        next_from_w[rr, :] = ghost
        add_w[rr, :] = face * (own - got)
        got = from_e[rr, :]
        mine = col_e[rr, :]
        ghost = next_from_e[rr, :] + moved(mine, LANES - both) * (got - mine)
        if r == 0:
            corner = c_se[...]
            beyond = pltpu.roll(moved(corner, LANES - both), 1, 0)
            ghost = ghost + jnp.where(sub == 0, beyond * (got - pltpu.roll(corner, 1, 0)), 0.0)
        if r == tiles - 1:
            ghost = ghost + jnp.where(sub == 7, moved(got, LANES - 2 * both) * pltpu.roll(c_ne[...], 7, 0), 0.0)
        next_from_e[rr, :] = ghost
        add_e[rr, :] = moved(mine, LANES - 2 * both) * got

    @pl.when(is_top)
    def _():
        fold_back.wait_recv()

        def ghosts(k, carry):
            rr = pl.ds(rows - 8, 8)
            ghost_w, ghost_e = next_from_w[rr, :], next_from_e[rr, :]
            for t in range(2):
                at = jnp.logical_and(sub == 7, lane == t * levels + k)
                value = jnp.broadcast_to(fb[k, pl.ds(8 + 2 * t + 1, 1), :], (8, LANES))
                ghost_w = ghost_w + jnp.where(at, moved(value, t * levels + k + 1), 0.0)
                value = jnp.broadcast_to(fb[k, pl.ds(12 + 2 * t, 1), :], (8, LANES))
                ghost_e = ghost_e + jnp.where(at, moved(value, t * levels + k), 0.0)
            next_from_w[rr, :] = ghost_w
            next_from_e[rr, :] = ghost_e
            for t in range(2):
                for l in range(2):
                    at = pl.ds(last, 1)
                    a1[t, k + 1, l, at, :] = a1[t, k + 1, l, at, :] + fb[k, pl.ds(2 * t + l, 1), :]
            return carry

        lax.fori_loop(0, levels, ghosts, 0)

    def complete(c, carry):
        for j in range(CHUNK):
            k = CHUNK * c + j
            at = pl.ds(k, 1)
            for l in range(2):
                nmb[k, l, pl.ds(first - 1, 1), :] = from_s[8 + l, at, :]
                for t in range(2):
                    i = 2 * t + l
                    low, high = pl.ds(first, 1), pl.ds(last, 1)
                    a1[t, k + 1, l, low, :] = a1[t, k + 1, l, low, :] + edge[i, at, :]
                    a1[t, k + 1, l, high, :] = a1[t, k + 1, l, high, :] + edge[4 + i, at, :]
                    a1[t, k + 1, l, pl.ds(first - 1, 1), :] = edge[8 + i, at, :]
                    a1[t, k + 1, l, pl.ds(last + 1, 1), :] = edge[12 + i, at, :]
            for r in range(tiles):
                rr, here = pl.ds(8 * r, 8), pl.ds(PAD + 8 * r, 8)
                for t in range(2):
                    q = t * levels + k
                    value = moved(add_w[rr, :], lax.rem(LANES - q, LANES))
                    a1[t, k + 1, 0, here, :] = a1[t, k + 1, 0, here, :] + jnp.where(at_first, value, 0.0)
                    value = moved(add_e[rr, :], LANES - 1 - q)
                    a1[t, k + 1, 1, here, :] = a1[t, k + 1, 1, here, :] + jnp.where(at_last, value, 0.0)
        return carry

    lax.fori_loop(0, chunks, complete, 0)

    def second_step(c, carry):
        for r in range(tiles):
            rr, here = pl.ds(8 * r, 8), pl.ds(PAD + 8 * r, 8)
            above, below = pl.ds(PAD + 8 * r + 1, 8), pl.ds(PAD + 8 * r - 1, 8)
            ghost_w, ghost_e, face_w = next_from_w[rr, :], next_from_e[rr, :], from_w[rr, :]
            for j in range(CHUNK):
                k = CHUNK * c + j
                for l in range(2):
                    cc = halves(l)
                    ce, cw, cn, cs = east_c[k, rr, cc], west_c[k, rr, cc], north_c[k, rr, cc], nmb[k, l, below, :]
                    cd, cu, cx = down_c[k + 1, rr, cc], down_c[k, rr, cc], diag_c[k, rr, cc]
                    if l == 0:
                        face = jnp.where(at_first, moved(face_w, LANES - both - k), 0.0)
                        cw, cx = cw + face, cx + face
                    if r == 0:
                        cx = cx + jnp.where(sub == 0, cs, 0.0)
                    for t in range(2):
                        q = t * levels + k
                        value = [a1[t, k + 1, m, here, :] for m in range(2)]
                        left_1 = moved(value[1], LANES - 1)
                        right_0 = moved(value[0], 1)
                        if l == 0:
                            to_e = jnp.where(at_last, left_1, moved(value[0], LANES - 1))
                            to_w = jnp.where(at_first, moved(ghost_w, lax.rem(LANES - q, LANES)), right_0)
                        else:
                            to_e = jnp.where(at_last, moved(ghost_e, LANES - 1 - q), left_1)
                            to_w = jnp.where(at_first, right_0, moved(value[1], 1))
                        total = (
                            cx * value[l]
                            + ce * to_e
                            - cw * to_w
                            + cn * a1[t, k + 1, l, above, :]
                            - cs * a1[t, k + 1, l, below, :]
                            + cd * a1[t, k + 2, l, here, :]
                            + cu * a1[t, k, l, here, :]
                        )
                        out[t, k, rr, cc] = total
        return carry

    lax.fori_loop(0, chunks, second_step, 0)

    @pl.when(is_top)
    def _():
        def add(k, carry):
            for t in range(2):
                for l in range(2):
                    at = pl.ds(rows - 1, 1)
                    out[t, k, at, halves(l)] = out[t, k, at, halves(l)] + fb[k, pl.ds(4 + 2 * t + l, 1), :]
            return carry

        lax.fori_loop(0, levels, add, 0)

    to_east.wait_send()
    to_west.wait_send()
    later_east.wait_send()
    later_west.wait_send()

    @pl.when(has_north)
    def _():
        to_north.wait_send()
        to_ne.wait_send()
        to_nw.wait_send()
        fold_load.wait()

    @pl.when(has_south)
    def _():
        to_south.wait_send()
        to_se.wait_send()
        to_sw.wait_send()

    @pl.when(is_top)
    def _():
        fold_out.wait_send()
        fold_back.wait_send()


def per_device(n_lon, n_lat, *args):
    _, levels, rows, cols = args[0].shape
    f32, i32 = jnp.float32, jnp.int32
    field = (levels, rows, cols)
    padded = (2, levels + 2, 2, rows + 2 * PAD, LANES)
    args = [pltpu.with_memory_space_constraint(value, pltpu.HBM) for value in args]
    column = (rows, LANES)
    return pl.pallas_call(
        functools.partial(kernel, n_lon, n_lat),
        out_shape=jax.ShapeDtypeStruct(args[0].shape, f32),
        in_specs=[pl.BlockSpec(memory_space=pltpu.HBM)] * 9,
        out_specs=pl.BlockSpec(memory_space=pltpu.VMEM),
        scratch_shapes=[
            pltpu.VMEM(padded, f32),
            pltpu.VMEM(padded, f32),
            pltpu.VMEM((levels, 2, rows + 2 * PAD, LANES), f32),
            *[pltpu.VMEM(field, f32) for _ in range(4)],
            *[pltpu.VMEM((rows, cols), i32) for _ in range(3)],
            pltpu.SMEM((cols,), i32),
            pltpu.VMEM((4, 2, levels, cols), f32),
            pltpu.VMEM((2, levels, cols), f32),
            pltpu.VMEM((3, levels, cols), f32),
            pltpu.VMEM((3, levels, cols), f32),
            pltpu.VMEM((2, levels, cols), f32),
            *[pltpu.VMEM(field, f32) for _ in range(4)],
            pltpu.VMEM((levels + 1, rows, cols), f32),
            pltpu.VMEM((14, levels, LANES), f32),
            pltpu.VMEM((9, levels, LANES), f32),
            pltpu.VMEM((14, levels, LANES), f32),
            pltpu.VMEM((9, levels, LANES), f32),
            pltpu.VMEM((rows + 8, LANES), f32),
            pltpu.VMEM(column, f32),
            pltpu.VMEM((rows + 8, LANES), f32),
            *[pltpu.VMEM(column, f32) for _ in range(5)],
            *[pltpu.VMEM((8, LANES), f32) for _ in range(4)],
            pltpu.VMEM((16, levels, LANES), f32),
            pltpu.VMEM(column, f32),
            pltpu.VMEM(column, f32),
            pltpu.VMEM((n_lon, 16, LANES), f32),
            pltpu.VMEM((n_lon, 16, LANES), f32),
            *[pltpu.VMEM((n_lon, 8, LANES), f32) for _ in range(4)],
            pltpu.VMEM((n_lon, 16, LANES), f32),
            pltpu.VMEM((n_lon, 16, LANES), f32),
            pltpu.SemaphoreType.DMA((18 + 6 * (levels // CHUNK),)),
            pltpu.SemaphoreType.DMA((10,)),
            pltpu.SemaphoreType.DMA((10,)),
            pltpu.SemaphoreType.DMA((2,)),
            pltpu.SemaphoreType.DMA((2,)),
        ],
        compiler_params=pltpu.CompilerParams(
            collective_id=0, has_side_effects=True, vmem_limit_bytes=32 * 1024 * 1024
        ),
    )(*args)


def solution(mesh):
    n_lon, n_lat = mesh.shape["lon"], mesh.shape["lat"]
    placed = (
        P(None, None, "lat", "lon"),
        P(None, "lat", "lon"),
        P(None, "lat", "lon"),
        P(None, "lat", "lon"),
        P(None, "lat", "lon"),
        P("lat", "lon"),
        P("lat", "lon"),
        P("lat", "lon"),
        P("lon"),
    )
    return jax.shard_map(
        functools.partial(per_device, n_lon, n_lat),
        mesh=mesh,
        in_specs=placed,
        out_specs=P(None, None, "lat", "lon"),
        check_vma=False,
    )
```

time: 236 us -> 24.3 us (0.10)
  blocking collectives: 127 us -> 0 us
  waiting for transfers between devices: 37.8 us -> 0 us
  starting transfers between devices: 28.8 us -> 0 us
  Pallas kernels: 0 us -> 23.2 us
  local copies, waits for them, and re-layouts: 21.6 us -> 0.97 us
  other arithmetic: 18.3 us -> 0 us
    all_gather x2 -> x0, blocking collectives: 127 us -> none  [per_device(): lax.all_gather(top_terms, 'lon', axis=1, tiled=True)]
    ppermute x8 -> x0, waiting for transfers between devices: 37.8 us -> none  [the longest x4 31.6 us: shifted(): return lax.ppermute(value, axis, pairs)]
    ppermute x8 -> x0, starting transfers between devices: 28.8 us -> none  [the longest x4 14.8 us: passed_along(): return lax.ppermute(array, axis, pairs)]
    pallas_call x0 -> x1, Pallas kernels: none -> 23.2 us  [per_device(): pl.pallas_call(functools.partial(kernel, n_lon, n_lat), out_shape=jax.Sha...]
    mul x8 -> x0, other arithmetic: 13.1 us -> none  [the longest x2 5.52 us: per_device(): masked = cell_open * tracer]
    slice x14 -> x0, local copies, waits for them, and re-layouts: 9.4 us -> none  [the longest x2 4.61 us: per_device(): north_push[:, :, :-1, :]]
    gather x2 -> x0, local copies, waits for them, and re-layouts: 4.63 us -> none  [select_partner(): picked = jnp.take(piece_rows, jnp.clip(partner_cols, 0, width - 1), axis=1)]
    add x1 -> x0, other arithmetic: 3.98 us -> none  [per_device(): tracer = result + jnp.where(top_row, returned, 0.0)]
  transfers between devices with their start and end apart: 8 -> 0, of which waited for: 5 -> 0; matrix products, arithmetic and copies ran while one was open for 9% -> 0% of each run, Pallas kernels for 0% -> 0%
where the time goes in v2:
time: 24.3 us; the launch traced here: 24.2 us
  Pallas kernels  23.2 us (95%)
  local copies, waits for them, and re-layouts  0.97 us (4%)
    pallas_call x1, Pallas kernels, per_device(): pl.pallas_call(functools.partial(kernel, n_lon, n_lat), out_shape=jax.Sha...  23.2 us
    unnamed x1, local copies, waits for them, and re-layouts  0.97 us

profile of v2, /device:TPU:1, one launch (start us, length us, event | category | flops | bytes accessed | tf_op | source)
XLA Modules:
  0.0 24.2 jit_solution(7863724536523635687)
XLA Ops:
  0.0 23.2 %shard_map.91 = f32[2,16,32,256]{3,2,1,0:T(8,128)S(1)} custom-call(f32[2,16,32,256]{3,2,1,0:T(8,128)} %ct.1, f32[16,32,256]{2,1,0:T(8,128)} %u_hbm.1, f32[16,32,256]{2,1,0:T(8,128)} %v_hbm.1, f32[16,32,256]{2,1,0:T(8,128)} %d_hbm.1, f32[16,32,256]{2,1,0:T(8,128)} %w_hbm.1, s32[32,256]{1,0:T(8,128)} %cm_hbm.1, s32[32,256]{1,0:T(8,128)} %em_hbm.1, ...), custom_call_target="tpu_custom_call" | custom-call | tf_op jit(solution)/shard_map/pallas_call | solution.py:656
  23.2 1.0 %copy.11 = f32[2,16,32,256]{3,2,1,0:T(8,128)} copy(f32[2,16,32,256]{3,2,1,0:T(8,128)S(1)} %shard_map.91) | data formatting | bytes 2097152

commit v3 on v2

--- a/solution.py
+++ b/solution.py
@@ -22,9 +22,9 @@
     east_c, west_c, north_c, diag_c, down_c,
     row_n, row_s, from_s, from_n,
     col_e, col_w, from_w, from_e, next_e, next_w, next_from_w, next_from_e,
-    c_sw, c_se, c_nw, c_ne,
-    edge, add_w, add_e,
-    fg, fq, fx, fy, f1, f2, fo, fb,
+    tiles_out, tiles_in, tiles_w, tiles_e,
+    edge, last_c, add_w, add_e,
+    fg, fq, fx, fy, gx, gy, f1, f2, fo, fb,
     load_sem, send_sem, recv_sem, fold_send, fold_recv,
 ):
     _, levels, rows, cols = ct.shape
@@ -57,14 +57,10 @@
     def _():
         greet((east, lat))
         greet((west, lat))
-        greet((east, lat + 1))
-        greet((west, lat + 1))
         greet((lon, lat + 1))
 
     @pl.when(has_south)
     def _():
-        greet((east, lat - 1))
-        greet((west, lat - 1))
         greet((lon, lat - 1))
 
     def load(src, dst, sem):
@@ -124,14 +120,12 @@
     @pl.when(is_bottom)
     def _():
         from_s[...] = jnp.zeros_like(from_s)
-        c_sw[...] = jnp.zeros_like(c_sw)
-        c_se[...] = jnp.zeros_like(c_se)
+        tiles_in[0] = jnp.zeros((levels, LANES), jnp.float32)
 
     @pl.when(is_top)
     def _():
         from_n[...] = jnp.zeros_like(from_n)
-        c_nw[...] = jnp.zeros_like(c_nw)
-        c_ne[...] = jnp.zeros_like(c_ne)
+        tiles_in[1] = jnp.zeros((levels, LANES), jnp.float32)
 
     lane = lax.broadcasted_iota(jnp.int32, (8, LANES), 1)
     sub = lax.broadcasted_iota(jnp.int32, (8, LANES), 0)
@@ -178,6 +172,8 @@
             diag = jnp.where(open_c[l], 1.0, 0.0) - plus[l] - north[l] - down[l] - up + side[l]
             if i == 1:
                 diag = diag + beyond[l]
+                last_c[l], last_c[2 + l], last_c[4 + l], last_c[6 + l] = diag, plus[l], side[l], down[l]
+                last_c[8 + l] = jnp.where(open_b[l], 0.5 * vr[1, :, halves(l)] + dr[1, :, halves(l)], 0.0)
             for t in range(2):
                 here = cell[t][:, halves(l)]
                 left = [moved(cell[t][:, halves(m)], LANES - 1) for m in range(2)]
@@ -199,18 +195,28 @@
             row_n[2 * t + l] = cell[t][:, halves(l)]
             row_n[4 + 2 * t + l] = result[t][l]
         row_n[8 + l] = south[l]
-        row_n[10 + l] = north[l]
-    row_n[12] = plus[1]
-    row_n[13] = minus[1]
+        row_n[12 + l] = north[l]
+    row_n[10] = plus[1]
+    row_n[11] = minus[1]
+
+    def corner_tile(cell, minus, plus, south):
+        tile = jnp.zeros((levels, LANES), jnp.float32)
+        for to, value, at in (
+            (0, cell[0][:, halves(0)], 0), (1, cell[1][:, halves(0)], 0), (2, south[0], 0),
+            (8, cell[0][:, halves(1)], LANES - 1), (9, cell[1][:, halves(1)], LANES - 1), (10, south[1], LANES - 1),
+            (11, minus[1], LANES - 1), (12, plus[1], LANES - 1),
+        ):
+            tile = jnp.where(row_lane == to, moved(value, (to - at) % LANES), tile)
+        return tile
+
+    tiles_out[0] = corner_tile(cell, minus, plus, south)
     cell, result, plus, minus, north, south = edge_row(0, 0)
     for l in range(2):
         for t in range(2):
             row_s[2 * t + l] = cell[t][:, halves(l)]
             row_s[4 + 2 * t + l] = result[t][l]
     row_s[8] = plus[1]
-
-    count = 2 + jnp.where(is_top, n_lon - 3, 3) + jnp.where(is_bottom, 0, 3)
-    pl.semaphore_wait(barrier, count)
+    tiles_out[1] = corner_tile(cell, minus, plus, south)
 
     def remote(src, dst, sem, at):
         return pltpu.make_async_remote_copy(
@@ -218,17 +224,18 @@
             device_id=at, device_id_type=MESH,
         )
 
-    to_north = remote(row_n.at[pl.ds(0, 13)], from_s.at[pl.ds(0, 13)], 0, (lon, lat + 1))
-    to_south = remote(row_s, from_n, 1, (lon, lat - 1))
+    to_north = remote(row_n.at[pl.ds(0, 10)], from_s.at[pl.ds(0, 10)], 0, (lon, lat + 1))
+    to_north_too = remote(row_n.at[pl.ds(12, 2)], from_s.at[pl.ds(12, 2)], 10, (lon, lat + 1))
+    to_south = remote(row_s.at[pl.ds(0, 8)], from_n.at[pl.ds(0, 8)], 1, (lon, lat - 1))
     to_east = remote(col_e, from_w, 2, (east, lat))
     to_west = remote(col_w, from_e, 3, (west, lat))
     later_east = remote(next_e, next_from_w, 4, (east, lat))
     later_west = remote(next_w, next_from_e, 5, (west, lat))
     tail = pl.ds(rows - 8, 8)
-    to_ne = remote(col_e.at[tail], c_sw, 6, (east, lat + 1))
-    to_nw = remote(col_w.at[tail], c_se, 7, (west, lat + 1))
-    to_se = remote(col_e.at[pl.ds(0, 8)], c_nw, 8, (east, lat - 1))
-    to_sw = remote(col_w.at[pl.ds(0, 8)], c_ne, 9, (west, lat - 1))
+    tile_north = remote(tiles_out.at[0], tiles_in.at[0], 6, (lon, lat + 1))
+    tile_south = remote(tiles_out.at[1], tiles_in.at[1], 7, (lon, lat - 1))
+    relay_east = remote(tiles_in, tiles_w, 8, (east, lat))
+    relay_west = remote(tiles_in, tiles_e, 9, (west, lat))
 
     def fold_copy(src, dst, sem, at):
         return pltpu.make_async_remote_copy(
@@ -237,27 +244,49 @@
         )
 
     some = pl.ds(0, n_lon - 1)
-    fold_out = fold_copy(fq.at[some], fg.at[some], 0, east)
-    fold_back = fold_copy(fo.at[some], fb.at[some], 1, east)
-
-    @pl.when(has_north)
-    def _():
-        to_north.start()
+    fold_out = fold_copy(fq.at[some, pl.ds(0, 12)], fg.at[some, pl.ds(0, 12)], 0, east)
+    fold_back = fold_copy(fo.at[some, pl.ds(0, 11)], fb.at[:, some, :], 1, east)
+
+    def first_sends():
+        count = 2 + jnp.where(is_top, n_lon - 3, 1) + jnp.where(is_bottom, 0, 1)
+        pl.semaphore_wait(barrier, count)
+
+        @pl.when(is_top)
+        def _():
+            others(lambda p: fold_copy(fq.at[p, pl.ds(0, 12)], fg.at[lon, pl.ds(0, 12)], 0, p).start())
+            fg[lon] = fq[lon]
+
+        @pl.when(has_north)
+        def _():
+            tile_north.start()
+            to_north.start()
+            to_north_too.start()
+
+        @pl.when(has_south)
+        def _():
+            tile_south.start()
+            to_south.start()
 
     @pl.when(is_top)
     def _():
         def collect(k, carry):
-            for i in range(14):
+            for i in range(12):
                 fq[k, pl.ds(i, 1), :] = row_n[i, pl.ds(k, 1), :]
             return carry
 
         lax.fori_loop(0, levels, collect, 0)
-        others(lambda p: fold_copy(fq.at[p], fg.at[lon], 0, p).start())
-        fg[lon] = fq[lon]
-
-    @pl.when(has_south)
-    def _():
-        to_south.start()
+
+    x, y = lax.rem(lon, 4), lax.rem(lat, 4)
+    ahead = jnp.logical_or(
+        jnp.logical_or(jnp.logical_and(y == 0, x <= 1), y == 1),
+        jnp.logical_or(jnp.logical_and(y == 2, x == 3), jnp.logical_and(y == 3, x >= 2)),
+    )
+    ahead = jnp.logical_or(ahead, jnp.logical_and(lat == 0, lon == n_lon - 1))
+    ahead = jnp.logical_and(ahead, jnp.logical_or(lon > 0, lat > 0))
+
+    @pl.when(jnp.logical_not(ahead))
+    def _():
+        first_sends()
 
     col_e[...] = jnp.zeros_like(col_e)
     col_w[...] = jnp.zeros_like(col_w)
@@ -331,48 +360,56 @@
     col_e[extra, :] = doubled(col_e[extra, :], (0,))
     col_w[tail, :] = doubled(col_w[tail, :], (both, 2 * both))
 
-    to_east.start()
-    to_west.start()
-
-    @pl.when(has_north)
-    def _():
-        to_ne.start()
-        to_nw.start()
-
-    @pl.when(has_south)
-    def _():
-        to_se.start()
-        to_sw.start()
-
-    def first_step(c, carry):
+    def column_sends():
+        to_east.start()
+        to_west.start()
+
+    @pl.when(jnp.logical_not(ahead))
+    def _():
+        column_sends()
+
+    def step_levels(c, buf, second):
         for r in range(tiles):
             rr, here = pl.ds(8 * r, 8), pl.ds(PAD + 8 * r, 8)
             above, below = pl.ds(PAD + 8 * r + 1, 8), pl.ds(PAD + 8 * r - 1, 8)
+            column = [
+                [[buf[t, CHUNK * c + j, l, here, :] for j in range(CHUNK + 2)] for l in range(2)] for t in range(2)
+            ]
+            downs = [[down_c[CHUNK * c + j, rr, halves(l)] for j in range(CHUNK + 1)] for l in range(2)]
+            if second:
+                ghost_w, ghost_e, face_w = next_from_w[rr, :], next_from_e[rr, :], from_w[rr, :]
             for j in range(CHUNK):
                 k = CHUNK * c + j
+                to_e, to_w = [], []
+                for t in range(2):
+                    q = t * levels + k
+                    value = [column[t][l][j + 1] for l in range(2)]
+                    left = [moved(x, LANES - 1) for x in value]
+                    right = [moved(x, 1) for x in value]
+                    edge_e = moved(ghost_e, LANES - 1 - q) if second else 0.0
+                    to_e.append([jnp.where(at_last, left[1], left[0]), jnp.where(at_last, edge_e, left[1])])
+                    edge_w = jnp.where(at_first, moved(ghost_w, lax.rem(LANES - q, LANES)), right[0]) if second else right[0]
+                    to_w.append([edge_w, jnp.where(at_first, right[0], right[1])])
                 for l in range(2):
                     cc = halves(l)
                     ce, cw, cn, cs = east_c[k, rr, cc], west_c[k, rr, cc], north_c[k, rr, cc], nmb[k, l, below, :]
-                    cd, cu, cx = down_c[k + 1, rr, cc], down_c[k, rr, cc], diag_c[k, rr, cc]
+                    cx = diag_c[k, rr, cc]
+                    if second and l == 0:
+                        face = jnp.where(at_first, moved(face_w, LANES - both - k), 0.0)
+                        cw, cx = cw + face, cx + face
+                    if second and r == 0:
+                        cx = cx + jnp.where(sub == 0, cs, 0.0)
                     for t in range(2):
-                        value = [a0[t, k + 1, m, here, :] for m in range(2)]
-                        left_1 = moved(value[1], LANES - 1)
-                        right_0 = moved(value[0], 1)
-                        if l == 0:
-                            to_e, to_w = jnp.where(at_last, left_1, moved(value[0], LANES - 1)), right_0
+                        total = cx * column[t][l][j + 1] + ce * to_e[t][l] - cw * to_w[t][l]
+                        total = total + (cn * buf[t, k + 1, l, above, :] - cs * buf[t, k + 1, l, below, :])
+                        total = total + (downs[l][j + 1] * column[t][l][j + 2] + downs[l][j] * column[t][l][j])
+                        if second:
+                            out[t, k, rr, cc] = total
                         else:
-                            to_e = jnp.where(at_last, 0.0, left_1)
-                            to_w = jnp.where(at_first, right_0, moved(value[1], 1))
-                        total = (
-                            cx * value[l]
-                            + ce * to_e
-                            - cw * to_w
-                            + cn * a0[t, k + 1, l, above, :]
-                            - cs * a0[t, k + 1, l, below, :]
-                            + cd * a0[t, k + 2, l, here, :]
-                            + cu * a0[t, k, l, here, :]
-                        )
-                        a1[t, k + 1, l, here, :] = total
+                            a1[t, k + 1, l, here, :] = total
+
+    def first_step(c, carry):
+        step_levels(c, a0, False)
         return carry
 
     lax.fori_loop(0, chunks, first_step, 0)
@@ -393,8 +430,24 @@
     for r in range(tiles):
         next_e[pl.ds(8 * r, 8), :] = packs[r]
         next_w[pl.ds(8 * r, 8), :] = packs[tiles + r]
+    @pl.when(ahead)
+    def _():
+        first_sends()
+        column_sends()
+
     later_east.start()
     later_west.start()
+
+    @pl.when(has_south)
+    def _():
+        tile_north.wait_recv()
+
+    @pl.when(has_north)
+    def _():
+        tile_south.wait_recv()
+
+    relay_east.start()
+    relay_west.start()
 
     even = jnp.bitwise_and(sub, 1) == 0
 
@@ -417,83 +470,67 @@
                 jnp.broadcast_to(fg[j, pl.ds(at + 1, 1), :], shape),
             )
 
-        def turn(j, value):
+        def turn(j, value, straight, swapped):
             turned = jnp.take_along_axis(value, source, axis=1, mode="promise_in_bounds")
-            fx[j] = turned
-            fy[j] = jnp.where(even, pltpu.roll(turned, 7, 0), pltpu.roll(turned, 1, 0))
-
-        def turned(i):
+            straight[j] = turned
+            swapped[j] = jnp.where(even, pltpu.roll(turned, 7, 0), pltpu.roll(turned, 1, 0))
+
+        def turned(i, straight, swapped):
             here = lax.rem(home + n_lon - i, n_lon)
             before = lax.rem(home + 2 * n_lon - i - 1, n_lon)
-            swapped = lax.rem(home + 2 * n_lon - i - 1 + odd, n_lon)
-            return jnp.where(keep, jnp.where(even, fx[here], fx[before]), fy[swapped])
-
-        for j in range(n_lon):
-            turn(j, -(faces(j, 8) * fg[j, pl.ds(0, 8), :]))
-        for i in range(n_lon):
-            f1[i] = turned(i)
+            third = lax.rem(home + 2 * n_lon - i - 1 + odd, n_lon)
+            return jnp.where(keep, jnp.where(even, straight[here], straight[before]), swapped[third])
+
+        low = sub < 4
         for j in range(n_lon):
             e, w = (j + 1) % n_lon, (j - 1) % n_lon
             own = fg[j, pl.ds(0, 8), :]
+            face = faces(j, 8)
             to_w = pltpu.roll(moved(fg[w, pl.ds(0, 8), :], 1), 7, 0)
             to_e = pltpu.roll(moved(fg[e, pl.ds(0, 8), :], LANES - 1), 1, 0)
-            face_w = moved(jnp.broadcast_to(fg[w, pl.ds(13, 1), :], (8, LANES)), 1)
-            face_e = jnp.broadcast_to(fg[j, pl.ds(12, 1), :], (8, LANES))
-            inner = pltpu.roll(own, 4, 0) + f1[j]
-            inner = inner + jnp.where(jnp.logical_and(even, at_first), face_w * (own - to_w), 0.0)
+            face_w = moved(jnp.broadcast_to(fg[w, pl.ds(11, 1), :], (8, LANES)), 1)
+            face_e = jnp.broadcast_to(fg[j, pl.ds(10, 1), :], (8, LANES))
+            inner = jnp.where(jnp.logical_and(even, at_first), face_w * (own - to_w), 0.0)
             inner = inner + jnp.where(jnp.logical_and(jnp.logical_not(even), at_last), face_e * to_e, 0.0)
-            f2[j] = -(faces(j, 8) * inner)
-        for j in range(n_lon):
-            turn(j, f2[j])
-        low = sub < 4
+            value = -(face * jnp.where(low, own, own + pltpu.roll(inner, 4, 0)))
+            f2[j] = value
+            turn(j, value, fx, fy)
+            turn(j, face, gx, gy)
+        for i in range(n_lon):
+            value = turned(i, fx, fy)
+            f1[i] = value
+            later = value - turned(i, gx, gy) * pltpu.roll(f2[i], 4, 0)
+            fo[i, pl.ds(0, 8), :] = jnp.where(low, value, later)
         for i in range(n_lon):
             e, w = (i + 1) % n_lon, (i - 1) % n_lon
-            fo[i, pl.ds(0, 8), :] = jnp.where(low, f1[i], pltpu.roll(turned(i), 4, 0))
-            fo[i, pl.ds(8, 8), :] = jnp.where(low, f1[w], pltpu.roll(f1[e], 4, 0))
-        others(lambda p: fold_copy(fo.at[p], fb.at[lon], 1, p).start())
-        fb[lon] = fo[lon]
+            fo[i, pl.ds(8, 8), :] = jnp.where(at_last, pltpu.roll(f1[w], 7, 0), f1[e])
+        others(lambda p: fold_copy(fo.at[p, pl.ds(0, 11)], fb.at[:, lon, :], 1, p).start())
+        for i in range(11):
+            fb[i, pl.ds(lon, 1), :] = fo[lon, pl.ds(i, 1), :]
 
     @pl.when(has_south)
     def _():
         to_north.wait_recv()
-        to_ne.wait_recv()
-        to_nw.wait_recv()
+        to_north_too.wait_recv()
 
     @pl.when(has_north)
     def _():
         to_south.wait_recv()
-        to_se.wait_recv()
-        to_sw.wait_recv()
 
     to_east.wait_recv()
     to_west.wait_recv()
     later_east.wait_recv()
     later_west.wait_recv()
 
-    def upright(ref, row, base):
-        spread = jnp.broadcast_to(ref[pl.ds(row, 1), :], (levels, LANES))
-        return jnp.sum(jnp.where(row_lane == row_level + base, spread, 0.0), axis=1, keepdims=True)
-
-    face_sw, face_nw = upright(c_sw, 7, both), upright(c_nw, 0, both)
     for t in range(2):
-        point = t * levels
         for l in range(2):
             at = 2 * t + l
             own, there = row_s[at], from_s[at]
             edge[at] = from_s[8 + l] * (own - there)
-            ghost = from_s[4 + at] + from_s[10 + l] * own
-            if l == 0:
-                ghost = ghost + jnp.where(row_first, face_sw * (there - upright(c_sw, 7, point)), 0.0)
-            else:
-                ghost = ghost + jnp.where(row_last, from_s[12] * upright(c_se, 7, point), 0.0)
-            edge[8 + at] = ghost
+            edge[8 + at] = from_s[4 + at] + from_s[12 + l] * own
             own, there = row_n[at], from_n[at]
-            edge[4 + at] = row_n[10 + l] * there
+            edge[4 + at] = row_n[12 + l] * there
             ghost = from_n[4 + at] + row_n[8 + l] * (there - own)
-            if l == 0:
-                ghost = ghost + jnp.where(row_first, face_nw * (there - upright(c_nw, 0, point)), 0.0)
-            else:
-                ghost = ghost + jnp.where(row_last, from_n[8] * upright(c_ne, 0, point), 0.0)
             edge[12 + at] = jnp.where(is_top, 0.0, ghost)
 
     for r in range(tiles):
@@ -502,48 +539,13 @@
         own = col_w[rr, :]
         face = moved(got, LANES - both)
         ghost = next_from_w[rr, :] + moved(got, LANES - 2 * both) * own
-        if r == 0:
-            corner = c_sw[...]
-            beyond = pltpu.roll(moved(corner, LANES - 3 * both), 1, 0)
-            ghost = ghost + jnp.where(sub == 0, beyond * (got - pltpu.roll(corner, 1, 0)), 0.0)
-        if r == tiles - 1:
-            ghost = ghost + jnp.where(sub == 7, from_w[extra, :] * pltpu.roll(c_nw[...], 7, 0), 0.0)
         next_from_w[rr, :] = ghost
         add_w[rr, :] = face * (own - got)
         got = from_e[rr, :]
         mine = col_e[rr, :]
         ghost = next_from_e[rr, :] + moved(mine, LANES - both) * (got - mine)
-        if r == 0:
-            corner = c_se[...]
-            beyond = pltpu.roll(moved(corner, LANES - both), 1, 0)
-            ghost = ghost + jnp.where(sub == 0, beyond * (got - pltpu.roll(corner, 1, 0)), 0.0)
-        if r == tiles - 1:
-            ghost = ghost + jnp.where(sub == 7, moved(got, LANES - 2 * both) * pltpu.roll(c_ne[...], 7, 0), 0.0)
         next_from_e[rr, :] = ghost
         add_e[rr, :] = moved(mine, LANES - 2 * both) * got
-
-    @pl.when(is_top)
-    def _():
-        fold_back.wait_recv()
-
-        def ghosts(k, carry):
-            rr = pl.ds(rows - 8, 8)
-            ghost_w, ghost_e = next_from_w[rr, :], next_from_e[rr, :]
-            for t in range(2):
-                at = jnp.logical_and(sub == 7, lane == t * levels + k)
-                value = jnp.broadcast_to(fb[k, pl.ds(8 + 2 * t + 1, 1), :], (8, LANES))
-                ghost_w = ghost_w + jnp.where(at, moved(value, t * levels + k + 1), 0.0)
-                value = jnp.broadcast_to(fb[k, pl.ds(12 + 2 * t, 1), :], (8, LANES))
-                ghost_e = ghost_e + jnp.where(at, moved(value, t * levels + k), 0.0)
-            next_from_w[rr, :] = ghost_w
-            next_from_e[rr, :] = ghost_e
-            for t in range(2):
-                for l in range(2):
-                    at = pl.ds(last, 1)
-                    a1[t, k + 1, l, at, :] = a1[t, k + 1, l, at, :] + fb[k, pl.ds(2 * t + l, 1), :]
-            return carry
-
-        lax.fori_loop(0, levels, ghosts, 0)
 
     def complete(c, carry):
         for j in range(CHUNK):
@@ -571,74 +573,106 @@
     lax.fori_loop(0, chunks, complete, 0)
 
     def second_step(c, carry):
-        for r in range(tiles):
-            rr, here = pl.ds(8 * r, 8), pl.ds(PAD + 8 * r, 8)
-            above, below = pl.ds(PAD + 8 * r + 1, 8), pl.ds(PAD + 8 * r - 1, 8)
-            ghost_w, ghost_e, face_w = next_from_w[rr, :], next_from_e[rr, :], from_w[rr, :]
+        step_levels(c, a1, True)
+        return carry
+
+    lax.fori_loop(0, chunks, second_step, 0)
+
+    relay_east.wait_recv()
+    relay_west.wait_recv()
+
+    def upright(ref, row, base):
+        spread = jnp.broadcast_to(ref[pl.ds(row, 1), :], (levels, LANES))
+        return jnp.sum(jnp.where(row_lane == row_level + base, spread, 0.0), axis=1, keepdims=True)
+
+    sw, nw, se, ne = tiles_w[0], tiles_w[1], tiles_e[0], tiles_e[1]
+
+    def lane_of(tile, at):
+        return tile[:, at : at + 1]
+
+    face_w = [upright(from_w, 0, both), upright(from_w, rows - 1, both)]
+    beyond_w, beyond_e = upright(from_w, rows + 7, 0), upright(from_e, rows - 1, 2 * both)
+    for t in range(2):
+        point = t * levels
+        there, above = from_s[2 * t], from_n[2 * t]
+        corner = lane_of(sw, 8 + t)
+        value = from_s[8] * (lane_of(sw, 11) * (there - corner))
+        value = value + face_w[0] * (lane_of(sw, 10) * (upright(from_w, 0, point) - corner))
+        edge[2 * t] = jnp.where(row_first, -value, 0.0)
+        corner = lane_of(se, t)
+        value = from_s[9] * (lane_of(tiles_in[0], 12) * corner)
+        value = row_s[8] * (lane_of(se, 2) * (upright(from_e, 0, point) - corner)) - value
+        edge[2 * t + 1] = jnp.where(row_last, value, 0.0)
+        corner = lane_of(nw, 8 + t)
+        value = row_n[12] * (lane_of(nw, 11) * (above - corner)) - face_w[1] * (beyond_w * corner)
+        edge[4 + 2 * t] = jnp.where(row_first, value, 0.0)
+        corner = lane_of(ne, t)
+        value = row_n[13] * (lane_of(tiles_in[1], 12) * corner) + row_n[10] * (beyond_e * corner)
+        edge[4 + 2 * t + 1] = jnp.where(row_last, value, 0.0)
+
+    def corners(c, carry):
+        for j in range(CHUNK):
+            k = CHUNK * c + j
+            for t in range(2):
+                for l in range(2):
+                    for i, row in ((2 * t + l, 0), (4 + 2 * t + l, rows - 1)):
+                        at = pl.ds(row, 1)
+                        out[t, k, at, halves(l)] = out[t, k, at, halves(l)] + edge[i, pl.ds(k, 1), :]
+        return carry
+
+    lax.fori_loop(0, chunks, corners, 0)
+
+    @pl.when(is_top)
+    def _():
+        fold_back.wait_recv()
+        for t in range(2):
+            value = [fb[2 * t + l] for l in range(2)]
+            beyond = fb[8 + 2 * t]
+            left = [moved(x, LANES - 1) for x in value]
+            right = [moved(x, 1) for x in value]
+            to_e = [jnp.where(row_last, left[1], left[0]), jnp.where(row_last, moved(beyond, LANES - 1), left[1])]
+            to_w = [jnp.where(row_first, moved(beyond, 1), right[0]), jnp.where(row_first, right[0], right[1])]
+            for l in range(2):
+                diag, side, down = last_c[l], last_c[4 + l], last_c[6 + l]
+                if l == 0:
+                    diag = diag + jnp.where(row_first, face_w[1], 0.0)
+                    side = side + jnp.where(row_first, face_w[1], 0.0)
+                total = diag * value[l] + last_c[2 + l] * to_e[l] - side * to_w[l]
+                total = total + down * pltpu.roll(value[l], levels - 1, 0)
+                total = total + pltpu.roll(down, 1, 0) * pltpu.roll(value[l], 1, 0)
+                edge[8 + 2 * t + l] = total + fb[4 + 2 * t + l]
+                edge[12 + 2 * t + l] = last_c[8 + l] * value[l]
+
+        def add(c, carry):
             for j in range(CHUNK):
                 k = CHUNK * c + j
-                for l in range(2):
-                    cc = halves(l)
-                    ce, cw, cn, cs = east_c[k, rr, cc], west_c[k, rr, cc], north_c[k, rr, cc], nmb[k, l, below, :]
-                    cd, cu, cx = down_c[k + 1, rr, cc], down_c[k, rr, cc], diag_c[k, rr, cc]
-                    if l == 0:
-                        face = jnp.where(at_first, moved(face_w, LANES - both - k), 0.0)
-                        cw, cx = cw + face, cx + face
-                    if r == 0:
-                        cx = cx + jnp.where(sub == 0, cs, 0.0)
-                    for t in range(2):
-                        q = t * levels + k
-                        value = [a1[t, k + 1, m, here, :] for m in range(2)]
-                        left_1 = moved(value[1], LANES - 1)
-                        right_0 = moved(value[0], 1)
-                        if l == 0:
-                            to_e = jnp.where(at_last, left_1, moved(value[0], LANES - 1))
-                            to_w = jnp.where(at_first, moved(ghost_w, lax.rem(LANES - q, LANES)), right_0)
-                        else:
-                            to_e = jnp.where(at_last, moved(ghost_e, LANES - 1 - q), left_1)
-                            to_w = jnp.where(at_first, right_0, moved(value[1], 1))
-                        total = (
-                            cx * value[l]
-                            + ce * to_e
-                            - cw * to_w
-                            + cn * a1[t, k + 1, l, above, :]
-                            - cs * a1[t, k + 1, l, below, :]
-                            + cd * a1[t, k + 2, l, here, :]
-                            + cu * a1[t, k, l, here, :]
-                        )
-                        out[t, k, rr, cc] = total
-        return carry
-
-    lax.fori_loop(0, chunks, second_step, 0)
-
-    @pl.when(is_top)
-    def _():
-        def add(k, carry):
-            for t in range(2):
-                for l in range(2):
-                    at = pl.ds(rows - 1, 1)
-                    out[t, k, at, halves(l)] = out[t, k, at, halves(l)] + fb[k, pl.ds(4 + 2 * t + l, 1), :]
+                for t in range(2):
+                    for l in range(2):
+                        for i, row in ((8 + 2 * t + l, rows - 1), (12 + 2 * t + l, rows - 2)):
+                            at = pl.ds(row, 1)
+                            out[t, k, at, halves(l)] = out[t, k, at, halves(l)] + edge[i, pl.ds(k, 1), :]
             return carry
 
-        lax.fori_loop(0, levels, add, 0)
+        lax.fori_loop(0, chunks, add, 0)
 
     to_east.wait_send()
     to_west.wait_send()
     later_east.wait_send()
     later_west.wait_send()
+    relay_east.wait_send()
+    relay_west.wait_send()
 
     @pl.when(has_north)
     def _():
         to_north.wait_send()
-        to_ne.wait_send()
-        to_nw.wait_send()
+        to_north_too.wait_send()
+        tile_north.wait_send()
         fold_load.wait()
 
     @pl.when(has_south)
     def _():
         to_south.wait_send()
-        to_se.wait_send()
-        to_sw.wait_send()
+        tile_south.wait_send()
 
     @pl.when(is_top)
     def _():
@@ -680,18 +714,19 @@
             pltpu.VMEM(column, f32),
             pltpu.VMEM((rows + 8, LANES), f32),
             *[pltpu.VMEM(column, f32) for _ in range(5)],
-            *[pltpu.VMEM((8, LANES), f32) for _ in range(4)],
+            *[pltpu.VMEM((2, levels, LANES), f32) for _ in range(4)],
             pltpu.VMEM((16, levels, LANES), f32),
+            pltpu.VMEM((10, levels, LANES), f32),
             pltpu.VMEM(column, f32),
             pltpu.VMEM(column, f32),
             pltpu.VMEM((n_lon, 16, LANES), f32),
             pltpu.VMEM((n_lon, 16, LANES), f32),
-            *[pltpu.VMEM((n_lon, 8, LANES), f32) for _ in range(4)],
+            *[pltpu.VMEM((n_lon, 8, LANES), f32) for _ in range(6)],
             pltpu.VMEM((n_lon, 16, LANES), f32),
-            pltpu.VMEM((n_lon, 16, LANES), f32),
+            pltpu.VMEM((11, n_lon, LANES), f32),
             pltpu.SemaphoreType.DMA((18 + 6 * (levels // CHUNK),)),
-            pltpu.SemaphoreType.DMA((10,)),
-            pltpu.SemaphoreType.DMA((10,)),
+            pltpu.SemaphoreType.DMA((11,)),
+            pltpu.SemaphoreType.DMA((11,)),
             pltpu.SemaphoreType.DMA((2,)),
             pltpu.SemaphoreType.DMA((2,)),
         ],

time: 24.3 us -> 21.3 us (0.88)
  Pallas kernels: 23.2 us -> 20.1 us
    pallas_call x1, Pallas kernels: 23.2 us -> 20.1 us  [per_device(): pl.pallas_call(functools.partial(kernel, n_lon, n_lat), out_shape=jax.Sha...]
where the time goes in v3:
time: 21.3 us; the launch traced here: 21.1 us
  Pallas kernels  20.1 us (94%)
  local copies, waits for them, and re-layouts  0.97 us (5%)
    pallas_call x1, Pallas kernels, per_device(): pl.pallas_call(functools.partial(kernel, n_lon, n_lat), out_shape=jax.Sha...  20.1 us
    unnamed x1, local copies, waits for them, and re-layouts  0.97 us

profile of v3, /device:TPU:1, one launch (start us, length us, event | category | flops | bytes accessed | tf_op | source)
XLA Modules:
  0.0 21.1 jit_solution(5933192282851643654)
XLA Ops:
  0.0 20.1 %shard_map.91 = f32[2,16,32,256]{3,2,1,0:T(8,128)S(1)} custom-call(f32[2,16,32,256]{3,2,1,0:T(8,128)} %ct.1, f32[16,32,256]{2,1,0:T(8,128)} %u_hbm.1, f32[16,32,256]{2,1,0:T(8,128)} %v_hbm.1, f32[16,32,256]{2,1,0:T(8,128)} %d_hbm.1, f32[16,32,256]{2,1,0:T(8,128)} %w_hbm.1, s32[32,256]{1,0:T(8,128)} %cm_hbm.1, s32[32,256]{1,0:T(8,128)} %em_hbm.1, ...), custom_call_target="tpu_custom_call" | custom-call | tf_op jit(solution)/shard_map/pallas_call | solution.py:690
  20.1 1.0 %copy.11 = f32[2,16,32,256]{3,2,1,0:T(8,128)} copy(f32[2,16,32,256]{3,2,1,0:T(8,128)S(1)} %shard_map.91) | data formatting | bytes 2097152

commit v4 on v3

--- a/solution.py
+++ b/solution.py
@@ -53,11 +53,18 @@
     def _():
         others(lambda p: greet((p, lat)))
 
+    origin = jnp.logical_and(lon == 0, lat == 0)
+    east_of = jnp.logical_and(lon == 1, lat == 0)
+    west_of = jnp.logical_and(lon == n_lon - 1, lat == 0)
+
     @pl.when(has_north)
+    def _():
+        greet((lon, lat + 1))
+
+    @pl.when(jnp.logical_and(has_north, jnp.logical_not(origin)))
     def _():
         greet((east, lat))
         greet((west, lat))
-        greet((lon, lat + 1))
 
     @pl.when(has_south)
     def _():
@@ -249,6 +256,7 @@
 
     def first_sends():
         count = 2 + jnp.where(is_top, n_lon - 3, 1) + jnp.where(is_bottom, 0, 1)
+        count = count - jnp.where(jnp.logical_or(east_of, west_of), 1, 0)
         pl.semaphore_wait(barrier, count)
 
         @pl.when(is_top)
@@ -276,12 +284,7 @@
 
         lax.fori_loop(0, levels, collect, 0)
 
-    x, y = lax.rem(lon, 4), lax.rem(lat, 4)
-    ahead = jnp.logical_or(
-        jnp.logical_or(jnp.logical_and(y == 0, x <= 1), y == 1),
-        jnp.logical_or(jnp.logical_and(y == 2, x == 3), jnp.logical_and(y == 3, x >= 2)),
-    )
-    ahead = jnp.logical_or(ahead, jnp.logical_and(lat == 0, lon == n_lon - 1))
+    ahead = jnp.logical_and(lat <= 1, jnp.logical_or(lon <= 1, lon == n_lon - 1))
     ahead = jnp.logical_and(ahead, jnp.logical_or(lon > 0, lat > 0))
 
     @pl.when(jnp.logical_not(ahead))
@@ -361,8 +364,13 @@
     col_w[tail, :] = doubled(col_w[tail, :], (both, 2 * both))
 
     def column_sends():
-        to_east.start()
-        to_west.start()
+        @pl.when(jnp.logical_not(west_of))
+        def _():
+            to_east.start()
+
+        @pl.when(jnp.logical_not(east_of))
+        def _():
+            to_west.start()
 
     @pl.when(jnp.logical_not(ahead))
     def _():
@@ -435,8 +443,13 @@
         first_sends()
         column_sends()
 
-    later_east.start()
-    later_west.start()
+    @pl.when(jnp.logical_not(west_of))
+    def _():
+        later_east.start()
+
+    @pl.when(jnp.logical_not(east_of))
+    def _():
+        later_west.start()
 
     @pl.when(has_south)
     def _():
@@ -446,8 +459,13 @@
     def _():
         tile_south.wait_recv()
 
-    relay_east.start()
-    relay_west.start()
+    @pl.when(jnp.logical_not(west_of))
+    def _():
+        relay_east.start()
+
+    @pl.when(jnp.logical_not(east_of))
+    def _():
+        relay_west.start()
 
     even = jnp.bitwise_and(sub, 1) == 0
 
@@ -508,6 +526,22 @@
         for i in range(11):
             fb[i, pl.ds(lon, 1), :] = fo[lon, pl.ds(i, 1), :]
 
+    to_east.wait_recv()
+
+    @pl.when(east_of)
+    def _():
+        to_west.start()
+        later_west.start()
+        relay_west.start()
+
+    to_west.wait_recv()
+
+    @pl.when(west_of)
+    def _():
+        to_east.start()
+        later_east.start()
+        relay_east.start()
+
     @pl.when(has_south)
     def _():
         to_north.wait_recv()
@@ -517,8 +551,6 @@
     def _():
         to_south.wait_recv()
 
-    to_east.wait_recv()
-    to_west.wait_recv()
     later_east.wait_recv()
     later_west.wait_recv()
 

time: 21.3 us -> 19.9 us (0.934)
  Pallas kernels: 20.1 us -> 18.7 us
    pallas_call x1, Pallas kernels: 20.1 us -> 18.7 us  [per_device(): pl.pallas_call(functools.partial(kernel, n_lon, n_lat), out_shape=jax.Sha...]
where the time goes in v4:
time: 19.9 us; the launch traced here: 19.7 us
  Pallas kernels  18.7 us (94%)
  local copies, waits for them, and re-layouts  0.97 us (5%)
    pallas_call x1, Pallas kernels, per_device(): pl.pallas_call(functools.partial(kernel, n_lon, n_lat), out_shape=jax.Sha...  18.7 us
    unnamed x1, local copies, waits for them, and re-layouts  0.97 us

profile of v4, /device:TPU:1, one launch (start us, length us, event | category | flops | bytes accessed | tf_op | source)
XLA Modules:
  0.0 19.7 jit_solution(10248607138505475037)
XLA Ops:
  0.0 18.7 %shard_map.91 = f32[2,16,32,256]{3,2,1,0:T(8,128)S(1)} custom-call(f32[2,16,32,256]{3,2,1,0:T(8,128)} %ct.1, f32[16,32,256]{2,1,0:T(8,128)} %u_hbm.1, f32[16,32,256]{2,1,0:T(8,128)} %v_hbm.1, f32[16,32,256]{2,1,0:T(8,128)} %d_hbm.1, f32[16,32,256]{2,1,0:T(8,128)} %w_hbm.1, s32[32,256]{1,0:T(8,128)} %cm_hbm.1, s32[32,256]{1,0:T(8,128)} %em_hbm.1, ...), custom_call_target="tpu_custom_call" | custom-call | tf_op jit(solution)/shard_map/pallas_call | solution.py:722
  18.7 1.0 %copy.11 = f32[2,16,32,256]{3,2,1,0:T(8,128)} copy(f32[2,16,32,256]{3,2,1,0:T(8,128)S(1)} %shard_map.91) | data formatting | bytes 2097152
